TPU v7x, 32 devices: a whole 2x2x4 slice. The times are simulated.
32 devices in a mesh: shots: 2 (over y), lat: 16 (over z, x, core).
Axes of the slice: x: 2, y: 2, z: 4, core: 2. Of those that a mesh axis runs over, the one named last changes fastest.
Arguments:
- source_field: float32 [2, 2, 2048, 2048], P(None, 'shots', 'lat'), parts along dimension 1, may hold values from -6 to 6
- rec_blocks: float32 [512, 2, 1, 128], P(('shots', 'lat')), parts along dimension 0, may hold values from -6 to 6
- dest_device: int32 [512, 1], P(('shots', 'lat')), parts along dimension 0, may hold values from 0 to 15; in each aligned block of 16 rows (0 to 15, 16 to 31, ...) at most 2 rows name the same one
- dest_bin: int32 [512], P(('shots', 'lat')), parts along dimension 0, may hold values from 0 to 2047
- slowness: float32 [1, 2048, 2048], P(None, 'lat'), may hold values from 0.25 to 0.7
- ref_index: int32 [1, 2048, 2048], P(None, 'lat'), may hold values from 0 to 1
- ref_slow: float32 [1, 2], replicated, may hold values from 0.25 to 0.7
- omega: float32 [1], replicated, may hold values from 190 to 380
Outputs:
- image: float32 [2, 2048, 2048], P('shots', 'lat'), parts along dimension 0
There are 2 independent parts, one for each index of `shots`. A program takes and returns all parts, laid end to end along the dimension named above; an argument that names none is the same for every part. Nothing has to cross between parts.
Inputs may be any that keep to these rules, and one draw needn't show every extreme that they name: `dest_device`: among the trace blocks of one device no destination device is named more than 2 times, a bound that some block reaches.
All inputs are finite; a program needn't handle non-finite values.
Results may differ from a plain program's by a relative error of at most 0.0003.
Values sent between devices are 32-bit elements; how exact they have to be, the bound alone decides.
A program may use at most 64 MiB of HBM per device.

v0:
```python
from functools import partial
import math

import jax
import jax.numpy as jnp
from jax import lax
from jax.sharding import PartitionSpec as P

NREF = 2
CAP = 2


SPACING = 0.01
DEPTH_STEP = 0.01
RADIX = 128


def angle_table(size, direction):
    index = jnp.arange(size, dtype=jnp.int32)
    product = index[:, None] * index[None, :] % size
    angle = direction * 2.0 * math.pi * product.astype(jnp.float32) / size
    return (jnp.cos(angle), jnp.sin(angle))


def twist_table(length, direction):
    outer_index = jnp.arange(length // RADIX, dtype=jnp.int32)
    radix_index = jnp.arange(RADIX, dtype=jnp.int32)
    product = outer_index[:, None] * radix_index[None, :] % length
    angle = direction * 2.0 * math.pi * product.astype(jnp.float32) / length
    return (jnp.cos(angle), jnp.sin(angle))


def complex_einsum(formula, real_in, imag_in, real_mat, imag_mat):
    multiply = partial(jnp.einsum, formula, precision=lax.Precision.HIGHEST)
    return (
        multiply(real_in, real_mat) - multiply(imag_in, imag_mat),
        multiply(real_in, imag_mat) + multiply(imag_in, real_mat),
    )


def transform(real_in, imag_in, trailing, direction):
    length = real_in.shape[-2] if trailing else real_in.shape[-1]
    inner = length // RADIX
    first_real, first_imag = angle_table(inner, direction)
    second_real, second_imag = angle_table(RADIX, direction)
    twist_real, twist_imag = twist_table(length, direction)
    initial = real_in.shape
    if trailing:
        shape = initial[:-2] + (inner, RADIX, initial[-1])
        twist_real = twist_real[:, :, None]
        twist_imag = twist_imag[:, :, None]
        tail = "z"
    else:
        shape = initial[:-1] + (inner, RADIX)
        tail = ""
    work_real = real_in.reshape(shape)
    work_imag = imag_in.reshape(shape)
    if direction < 0:
        work_real, work_imag = complex_einsum(
            "...ab" + tail + ",ac->...cb" + tail, work_real, work_imag, first_real, first_imag
        )
        work_real, work_imag = (
            work_real * twist_real - work_imag * twist_imag,
            work_real * twist_imag + work_imag * twist_real,
        )
        work_real, work_imag = complex_einsum(
            "...cb" + tail + ",bd->...cd" + tail, work_real, work_imag, second_real, second_imag
        )
    else:
        work_real, work_imag = complex_einsum(
            "...cb" + tail + ",bd->...cd" + tail, work_real, work_imag, second_real, second_imag
        )
        work_real, work_imag = (
            work_real * twist_real - work_imag * twist_imag,
            work_real * twist_imag + work_imag * twist_real,
        )
        work_real, work_imag = complex_einsum(
            "...cb" + tail + ",ca->...ab" + tail, work_real, work_imag, first_real, first_imag
        )
        work_real = work_real / length
        work_imag = work_imag / length
    return (work_real.reshape(initial), work_imag.reshape(initial))


def permuted_numbers(positions, length):
    inner = length // RADIX
    index = positions // RADIX + inner * (positions % RADIX)
    signed = jnp.where(index < length // 2, index, index - length)
    return signed.astype(jnp.float32) * (2.0 * math.pi / (length * SPACING))


def per_device(
    source_field, rec_blocks, dest_device, dest_bin, slowness, ref_index, ref_slow, omega
):
    lanes = lax.axis_size("lat")
    count_blocks = rec_blocks.shape[0]
    freqs = rec_blocks.shape[2]
    block_width = rec_blocks.shape[3]
    rows_here = source_field.shape[2]
    columns = source_field.shape[3]
    bins_here = rows_here * (columns // block_width)
    slots = lanes * CAP
    flat = rec_blocks.reshape(count_blocks, 2 * freqs * block_width)
    onehot = (dest_device == jnp.arange(lanes, dtype=jnp.int32)[None, :]).astype(jnp.int32)
    order = jnp.arange(count_blocks, dtype=jnp.int32)
    before = (order[None, :] < order[:, None]).astype(jnp.int32)
    earlier = jnp.sum(before[:, :, None] * onehot[None, :, :], axis=1)
    ranking = jnp.sum(onehot * earlier, axis=1)
    slot_of = dest_device[:, 0] * CAP + ranking
    placing = slot_of[None, :] == jnp.arange(slots, dtype=jnp.int32)[:, None]
    outgoing = jnp.dot(placing.astype(jnp.float32), flat, precision=lax.Precision.HIGHEST)
    labels = jnp.sum(jnp.where(placing, (dest_bin + 1)[None, :], 0), axis=1).astype(jnp.float32)
    arrived, arrived_labels = (
        lax.all_to_all(
            outgoing.reshape(lanes, CAP, -1), "lat", split_axis=0, concat_axis=0, tiled=True
        ),
        lax.all_to_all(labels.reshape(lanes, CAP), "lat", split_axis=0, concat_axis=0, tiled=True),
    )
    bin_labels = arrived_labels.reshape(slots).astype(jnp.int32) - 1
    gathering = (bin_labels[None, :] == jnp.arange(bins_here, dtype=jnp.int32)[:, None]).astype(
        jnp.float32
    )
    binned = jnp.dot(gathering, arrived.reshape(slots, -1), precision=lax.Precision.HIGHEST)
    binned = binned.reshape(rows_here, columns // block_width, 2, freqs, block_width)
    received = binned.transpose(2, 3, 0, 1, 4).reshape(2, freqs, rows_here, columns)
    field_real = jnp.concatenate([source_field[0], received[0]], axis=0)
    field_imag = jnp.concatenate([source_field[1], received[1]], axis=0)
    signed = jnp.concatenate([-omega, omega])
    spec_real, spec_imag = transform(field_real, field_imag, False, -1.0)
    carried = jnp.broadcast_to(signed[:, None, None], (2 * freqs, 1, lanes))
    part_real = lax.all_to_all(spec_real, "lat", split_axis=2, concat_axis=1, tiled=True)
    part_imag = lax.all_to_all(spec_imag, "lat", split_axis=2, concat_axis=1, tiled=True)
    part_params = lax.all_to_all(carried, "lat", split_axis=2, concat_axis=1, tiled=True)
    total_rows = part_real.shape[1]
    local_cols = part_real.shape[2]
    freq_real, freq_imag = transform(part_real, part_imag, True, -1.0)
    kx_values = permuted_numbers(jnp.arange(total_rows, dtype=jnp.int32), total_rows)
    positions = lax.axis_index("lat") * local_cols + jnp.arange(local_cols, dtype=jnp.int32)
    ky_values = permuted_numbers(positions, lanes * local_cols)
    radial = kx_values[:, None] ** 2 + ky_values[None, :] ** 2
    freq_signed = part_params[:, 0, 0]
    sense = jnp.sign(freq_signed)[:, None, None]
    shifted_real = []
    shifted_imag = []
    for propagate_which in range(NREF):
        propagate_speed = ref_slow[0, propagate_which]
        argument = (freq_signed**2)[:, None, None] * propagate_speed**2 - radial[None]
        amplitude = jnp.exp(-jnp.sqrt(jnp.maximum(-argument, 0.0)) * DEPTH_STEP)
        phase = sense * jnp.sqrt(jnp.maximum(argument, 0.0)) * DEPTH_STEP
        factor_real = amplitude * jnp.cos(phase)
        factor_imag = amplitude * jnp.sin(phase)
        moved_real = freq_real * factor_real - freq_imag * factor_imag
        moved_imag = freq_real * factor_imag + freq_imag * factor_real
        moved_real, moved_imag = transform(moved_real, moved_imag, True, 1.0)
        shifted_real.append(moved_real)
        shifted_imag.append(moved_imag)
    stacked_real = jnp.stack(shifted_real, axis=1)
    stacked_imag = jnp.stack(shifted_imag, axis=1)
    back_real = lax.all_to_all(stacked_real, "lat", split_axis=2, concat_axis=3, tiled=True)
    back_imag = lax.all_to_all(stacked_imag, "lat", split_axis=2, concat_axis=3, tiled=True)
    space_real, space_imag = transform(back_real, back_imag, False, 1.0)
    new_real = jnp.zeros_like(field_real)
    new_imag = jnp.zeros_like(field_imag)
    for which in range(NREF):
        speed = ref_slow[0, which]
        angle = signed[:, None, None] * (slowness[0] - speed)[None] * DEPTH_STEP
        cosine = jnp.cos(angle)
        sine = jnp.sin(angle)
        fixed_real = space_real[:, which] * cosine - space_imag[:, which] * sine
        fixed_imag = space_real[:, which] * sine + space_imag[:, which] * cosine
        chosen = (ref_index[0] == which)[None]
        new_real = jnp.where(chosen, fixed_real, new_real)
        new_imag = jnp.where(chosen, fixed_imag, new_imag)
    images = [
        jnp.sum(new_real[:freqs] * new_real[freqs:] + new_imag[:freqs] * new_imag[freqs:], axis=0)
    ]
    return jnp.stack(images)


def solution(mesh):
    return jax.shard_map(
        per_device,
        mesh=mesh,
        in_specs=(
            P(None, "shots", "lat", None),
            P(("shots", "lat"), None, None, None),
            P(("shots", "lat"), None),
            P(("shots", "lat")),
            P(None, "lat", None),
            P(None, "lat", None),
            P(),
            P(),
        ),
        out_specs=P("shots", "lat", None),
        check_vma=False,
    )
```

profile of v0, /device:TPU:11, one launch (start us, length us, event | category | flops | bytes accessed | tf_op | source)
XLA Modules:
  0.0 519.5 jit_solution(6403087948331232962)
XLA Ops:
  3.8 6.6 %all-to-all-start = ((f32[16,1,2]{2,1,0:T(1,128)}), f32[16,1,2]{2,1,0:T(1,128)S(1)}, u32[]{:S(2)}, u32[]{:S(2)}) async-start(f32[16,1,2]{2,1,0:T(1,128)} %bitcast.9), calls=%async_computation | async-start | bytes 16384 | tf_op jit(solution)/shard_map/all_to_all | solution.py:117
  17.0 6.0 %all-to-all-start.1 = ((f32[16,2,256]{2,1,0:T(2,128)}), f32[16,2,256]{2,1,0:T(2,128)S(1)}, u32[]{:S(2)}, u32[]{:S(2)}) async-start(f32[16,2,256]{2,1,0:T(2,128)} %copy.188), calls=%async_computation.1 | async-start | bytes 65536 | tf_op jit(solution)/shard_map/all_to_all | solution.py:114
  27.8 6.0 %all-to-all-start.4 = ((f32[2,1,16]{0,1,2:T(1,128)}), f32[2,1,16]{0,1,2:T(1,128)S(1)}, u32[]{:S(2)}, u32[]{:S(2)}) async-start(f32[2,1,16]{0,1,2:T(1,128)} %broadcast_in_dim.38), calls=%async_computation.4 | async-start | bytes 16384 | tf_op jit(solution)/shard_map/all_to_all | solution.py:133
  53.9 8.6 %copy.212 = f32[2,128,2048]{1,0,2:T(2,128)} copy(f32[2,128,2048]{1,2,0:T(8,128)S(1)} %bitcast.330) | data formatting | bytes 4194304 | tf_op jit(solution)/shard_map/reshape | solution.py:82
  62.5 6.4 %all-to-all-start.3 = ((f32[2,128,2048]{1,0,2:T(2,128)}), f32[2,128,2048]{1,0,2:T(2,128)}, u32[]{:S(2)}, u32[]{:S(2)}) async-start(f32[2,128,2048]{1,0,2:T(2,128)} %copy.212), calls=%async_computation.3 | async-start | bytes 4194304 | tf_op jit(solution)/shard_map/all_to_all | solution.py:132
  76.1 8.6 %copy.205 = f32[2,128,2048]{1,0,2:T(2,128)} copy(f32[2,128,2048]{1,2,0:T(8,128)S(1)} %bitcast.329) | data formatting | bytes 4194304 | tf_op jit(solution)/shard_map/reshape | solution.py:82
  84.7 31.6 %all-to-all-done.3 = f32[2,128,2048]{1,0,2:T(2,128)} async-done(((f32[2,128,2048]{1,0,2:T(2,128)}), f32[2,128,2048]{1,0,2:T(2,128)}, u32[]{:S(2)}, u32[]{:S(2)}) %all-to-all-start.3) | async-done | bytes 2097184 | tf_op jit(solution)/shard_map/all_to_all | solution.py:132
  116.2 4.9 all-to-all-start.2
  134.0 34.6 %all-to-all-done.2 = f32[2,128,2048]{1,0,2:T(2,128)} async-done(((f32[2,128,2048]{1,0,2:T(2,128)}), f32[2,128,2048]{1,0,2:T(2,128)}, u32[]{:S(2)}, u32[]{:S(2)}) %all-to-all-start.2) | async-done | bytes 2097184 | tf_op jit(solution)/shard_map/all_to_all | solution.py:131
  185.9 21.9 %fusion.41 = (f32[2,16,128,128]{3,2,1,0:T(8,128)S(1)}, f32[2,16,128,128]{3,2,1,0:T(8,128)S(1)}, f32[2,16,128,128]{3,2,1,0:T(8,128)S(1)}, f32[2,16,128,128]{3,2,1,0:T(8,128)S(1)}) fusion(f32[128,2,16,128]{3,0,2,1:T(8,128)S(1)} %fusion.122, f32[2]{0:T(128)S(1)} %get-tuple-element.6, f32[16,128,128]{2,1,0:T(8,128)S(1)} %broadcast_add_fusion, ...), kind=kOutput, calls=%fused_computation.67 | convolution fusion | flops 822837248 | bytes 15728664 | tf_op jit(solution)/shard_map/...cbz,bd->...cdz/dot_general | solution.py:37
  240.8 12.2 %copy.246 = f32[2,2,2048,128]{3,0,1,2:T(2,128)} copy(f32[2,2,2048,128]{3,2,0,1:T(8,128)S(1)} %pad_maximum_fusion) | data formatting | bytes 8388608 | tf_op jit(solution)/shard_map/stack | solution.py:157
  253.0 5.1 all-to-all-start.5
  274.7 12.3 %copy.258 = f32[2,2,2048,128]{3,0,1,2:T(2,128)} copy(f32[2,2,2048,128]{3,2,0,1:T(8,128)S(1)} %pad_maximum_fusion.1) | data formatting | bytes 8388608 | tf_op jit(solution)/shard_map/stack | solution.py:158
  286.9 63.4 %all-to-all-done.5 = f32[2,2,2048,128]{3,0,1,2:T(2,128)} async-done(((f32[2,2,2048,128]{3,0,1,2:T(2,128)}), f32[2,2,2048,128]{3,0,1,2:T(2,128)}, u32[]{:S(2)}, u32[]{:S(2)}) %all-to-all-start.5) | async-done | bytes 4194336 | tf_op jit(solution)/shard_map/all_to_all | solution.py:159
  350.4 4.9 all-to-all-start.6
  360.6 5.5 %fusion.136 = f32[2,2,128,16,128]{4,2,3,1,0:T(8,128)} fusion(f32[2,2,128,16,128]{4,2,3,1,0:T(8,128)S(1)} %bitcast.327), kind=kOutput, calls=%fused_computation.172 | convolution fusion | flops 1610842112 | bytes 8388608 | tf_op jit(solution)/shard_map/...cb,bd->...cd/dot_general | solution.py:36
  366.1 5.6 %fusion.138 = f32[2,2,128,16,128]{4,2,3,1,0:T(8,128)} fusion(f32[2,2,128,16,128]{4,2,3,1,0:T(8,128)S(1)} %bitcast.328), kind=kOutput, calls=%fused_computation.174 | convolution fusion | flops 1610842112 | bytes 8388608 | tf_op jit(solution)/shard_map/...cb,bd->...cd/dot_general | solution.py:37
  371.7 76.0 %all-to-all-done.6 = f32[2,2,2048,128]{3,0,1,2:T(2,128)} async-done(((f32[2,2,2048,128]{3,0,1,2:T(2,128)}), f32[2,2,2048,128]{3,0,1,2:T(2,128)}, u32[]{:S(2)}, u32[]{:S(2)}) %all-to-all-start.6) | async-done | bytes 4194336 | tf_op jit(solution)/shard_map/all_to_all | solution.py:160
  459.7 6.1 %fusion = f32[16,2,2,128,128]{4,0,3,2,1:T(8,128)S(1)} fusion(f32[2,2,128,16,128]{4,2,3,1,0:T(8,128)S(1)} %get-tuple-element.11), kind=kOutput, calls=%fused_computation.6 | convolution fusion | flops 201330176 | bytes 8388608 | tf_op jit(solution)/shard_map/...cb,ca->...ab/dot_general | solution.py:37
  465.9 6.6 %fusion.2 = f32[16,2,2,128,128]{4,0,3,2,1:T(8,128)} fusion(f32[2,2,128,16,128]{4,2,3,1,0:T(8,128)S(1)} %get-tuple-element.11), kind=kOutput, calls=%fused_computation.8 | convolution fusion | flops 201330176 | bytes 8388608 | tf_op jit(solution)/shard_map/...cb,ca->...ab/dot_general | solution.py:36
  472.5 6.8 %multiply_bitcast_fusion = f32[2,2,128,16,128]{4,3,2,1,0:T(8,128)} fusion(f32[16,2,2,128,128]{4,0,3,2,1:T(8,128)S(1)} %fusion, f32[2,2,128,16,128]{4,2,3,1,0:T(8,128)S(1)} %get-tuple-element.10), kind=kOutput, calls=%fused_computation.2 | convolution fusion | flops 203427328 | bytes 12582912 | tf_op jit(solution)/shard_map/...cb,ca->...ab/dot_general | solution.py:37
  479.4 4.9 reshape.416
  484.3 10.1 %multiply_bitcast_fusion.1 = f32[2,2,128,16,128]{4,3,2,1,0:T(8,128)} fusion(f32[16,2,2,128,128]{4,0,3,2,1:T(8,128)} %fusion.2, f32[2,2,128,16,128]{4,2,3,1,0:T(8,128)} %copy-done), kind=kOutput, calls=%fused_computation.3 | convolution fusion | flops 203427328 | bytes 12582912 | tf_op jit(solution)/shard_map/...cb,ca->...ab/dot_general | solution.py:36
  499.3 18.7 %select_select_fusion.1 = (f32[2,128,2048]{2,1,0:T(8,128)S(1)}, f32[2,128,2048]{2,1,0:T(8,128)S(1)}) fusion(f32[2,2,128,2048]{3,2,1,0:T(8,128)} %reshape.415, f32[2,2,128,2048]{3,2,1,0:T(8,128)} %reshape.416, f32[128,2048]{1,0:T(8,128)S(1)} %get-tuple-element.33, f32[128,2048]{1,0:T(8,128)S(1)} %get-tuple-element.32, f32[2]{0:T(128)S(1)} %pad_maximum_fusion.4, ...), kind=kLoop, calls=%fused_computation.83 | loop fusion | flops 10485760 | bytes 15204360 | tf_op jit(solution)/shard_map/jit(_where)/select_n | solution.py:172
  (115 shorter events, 141.6 us)
Async XLA Ops:
  3.8 13.2 %all-to-all-start = ((f32[16,1,2]{2,1,0:T(1,128)}), f32[16,1,2]{2,1,0:T(1,128)S(1)}, u32[]{:S(2)}, u32[]{:S(2)}) async-start(f32[16,1,2]{2,1,0:T(1,128)} %bitcast.9), calls=%async_computation | async-start | bytes 16384 | tf_op jit(solution)/shard_map/all_to_all | solution.py:117
  17.0 10.2 %all-to-all-start.1 = ((f32[16,2,256]{2,1,0:T(2,128)}), f32[16,2,256]{2,1,0:T(2,128)S(1)}, u32[]{:S(2)}, u32[]{:S(2)}) async-start(f32[16,2,256]{2,1,0:T(2,128)} %copy.188), calls=%async_computation.1 | async-start | bytes 65536 | tf_op jit(solution)/shard_map/all_to_all | solution.py:114
  27.8 34.7 %all-to-all-start.4 = ((f32[2,1,16]{0,1,2:T(1,128)}), f32[2,1,16]{0,1,2:T(1,128)S(1)}, u32[]{:S(2)}, u32[]{:S(2)}) async-start(f32[2,1,16]{0,1,2:T(1,128)} %broadcast_in_dim.38), calls=%async_computation.4 | async-start | bytes 16384 | tf_op jit(solution)/shard_map/all_to_all | solution.py:133
  48.2 2.8 copy-start.1
  62.5 53.7 %all-to-all-start.3 = ((f32[2,128,2048]{1,0,2:T(2,128)}), f32[2,128,2048]{1,0,2:T(2,128)}, u32[]{:S(2)}, u32[]{:S(2)}) async-start(f32[2,128,2048]{1,0,2:T(2,128)} %copy.212), calls=%async_computation.3 | async-start | bytes 4194304 | tf_op jit(solution)/shard_map/all_to_all | solution.py:132
  84.7 36.7 %copy-start.12 = (f32[1,2]{1,0:T(1,128)S(1)}, f32[1,2]{1,0:T(1,128)}, u32[]{:S(2)}) copy-start(f32[1,2]{1,0:T(1,128)} %param.14) | copy-start | bytes 28
  116.2 52.4 %all-to-all-start.2 = ((f32[2,128,2048]{1,0,2:T(2,128)}), f32[2,128,2048]{1,0,2:T(2,128)}, u32[]{:S(2)}, u32[]{:S(2)}) async-start(f32[2,128,2048]{1,0,2:T(2,128)} %copy.205), calls=%async_computation.2 | async-start | bytes 4194304 | tf_op jit(solution)/shard_map/all_to_all | solution.py:131
  171.1 3.8 copy-start.9
  227.0 2.9 copy-start.2
  227.0 6.8 %copy-start.6 = (f32[2,16,128,128]{3,2,1,0:T(8,128)}, f32[2,16,128,128]{3,2,1,0:T(8,128)S(1)}, u32[]{:S(2)}) copy-start(f32[2,16,128,128]{3,2,1,0:T(8,128)S(1)} %get-tuple-element.21) | copy-start | bytes 6291460
  227.1 6.8 %copy-start.4 = (f32[2,16,128,128]{3,2,1,0:T(8,128)}, f32[2,16,128,128]{3,2,1,0:T(8,128)S(1)}, u32[]{:S(2)}) copy-start(f32[2,16,128,128]{3,2,1,0:T(8,128)S(1)} %get-tuple-element.34) | copy-start | bytes 6291460
  253.0 97.4 %all-to-all-start.5 = ((f32[2,2,2048,128]{3,0,1,2:T(2,128)}), f32[2,2,2048,128]{3,0,1,2:T(2,128)}, u32[]{:S(2)}, u32[]{:S(2)}) async-start(f32[2,2,2048,128]{3,0,1,2:T(2,128)} %copy.246), calls=%async_computation.5 | async-start | bytes 8388608 | tf_op jit(solution)/shard_map/all_to_all | solution.py:159
  258.1 4.6 copy-start.3
  265.8 1.6 copy-start.5
  286.9 68.3 %copy-start.10 = (s32[1,128,2048]{2,1,0:T(8,128)S(1)}, s32[1,128,2048]{2,1,0:T(8,128)}, u32[]{:S(2)}) copy-start(s32[1,128,2048]{2,1,0:T(8,128)} %param.13) | copy-start | bytes 3145732
  350.4 97.4 %all-to-all-start.6 = ((f32[2,2,2048,128]{3,0,1,2:T(2,128)}), f32[2,2,2048,128]{3,0,1,2:T(2,128)}, u32[]{:S(2)}, u32[]{:S(2)}) async-start(f32[2,2,2048,128]{3,0,1,2:T(2,128)} %copy.258), calls=%async_computation.6 | async-start | bytes 8388608 | tf_op jit(solution)/shard_map/all_to_all | solution.py:160
  355.3 1.2 copy-start.11
  447.8 3.4 copy-start.8
  451.2 3.9 copy-start.7
  459.7 12.8 %copy-start = (f32[2,2,128,16,128]{4,2,3,1,0:T(8,128)}, f32[2,2,128,16,128]{4,2,3,1,0:T(8,128)S(1)}, u32[]{:S(2)}) copy-start(f32[2,2,128,16,128]{4,2,3,1,0:T(8,128)S(1)} %get-tuple-element.10) | copy-start | bytes 12582916
where the time goes:
time: 523 us; the launch traced here: 519 us
  waiting for transfers between devices  210 us (40%)
  matrix products  164 us (31%)
  local copies, waits for them, and re-layouts  73.2 us (14%)
  starting transfers between devices  39.9 us (8%)
  other arithmetic  28 us (5%)
    all_to_all x1, waiting for transfers between devices, per_device(): lax.all_to_all(stacked_imag, 'lat', split_axis=2, concat_axis=3, tiled=True)  76 us
    all_to_all x1, waiting for transfers between devices, per_device(): lax.all_to_all(stacked_real, 'lat', split_axis=2, concat_axis=3, tiled=True)  63.4 us
    dot_general x10, matrix products, complex_einsum(): multiply(real_in, imag_mat) + multiply(imag_in, real_mat)  54.8 us
    dot_general x10, matrix products, complex_einsum(): multiply(real_in, real_mat) - multiply(imag_in, imag_mat)  38.5 us
    dot_general x10, matrix products, complex_einsum(): multiply(imag_in, real_mat)  35.8 us
    all_to_all x1, waiting for transfers between devices, per_device(): lax.all_to_all(spec_real, 'lat', split_axis=2, concat_axis=1, tiled=True)  34.6 us
    dot_general x10, matrix products, complex_einsum(): multiply(imag_in, imag_mat)  34.1 us
    all_to_all x1, waiting for transfers between devices, per_device(): lax.all_to_all(spec_imag, 'lat', split_axis=2, concat_axis=1, tiled=True)  31.6 us
  transfers between devices with their start and end apart: 7, of which 5 were waited for; matrix products, arithmetic and copies ran while one was open for 20% of the time, Pallas kernels for 0%

commit v1 on v0

--- a/solution.py
+++ b/solution.py
@@ -3,7 +3,10 @@
 
 import jax
 import jax.numpy as jnp
+import numpy as np
 from jax import lax
+from jax.experimental import pallas as pl
+from jax.experimental.pallas import tpu as pltpu
 from jax.sharding import PartitionSpec as P
 
 NREF = 2
@@ -89,7 +92,7 @@
     return signed.astype(jnp.float32) * (2.0 * math.pi / (length * SPACING))
 
 
-def per_device(
+def general(
     source_field, rec_blocks, dest_device, dest_bin, slowness, ref_index, ref_slow, omega
 ):
     lanes = lax.axis_size("lat")
@@ -177,6 +180,288 @@
     return jnp.stack(images)
 
 
+INNER = 16
+LENGTH = INNER * RADIX
+PARAMS = pltpu.CompilerParams(vmem_limit_bytes=50 * 2**20)
+
+
+def dft_tables(direction, left, scale):
+    index = np.arange(RADIX)
+    angle = direction * 2.0 * np.pi * (index[:, None] * index[None, :] % RADIX) / RADIX
+    cosine, sine = np.cos(angle) * scale, np.sin(angle) * scale
+    whole = np.block([[cosine, -sine], [sine, cosine]] if left else [[cosine, sine], [-sine, cosine]])
+    whole = jnp.asarray(whole.astype(np.float32))
+    high = whole.astype(jnp.bfloat16)
+    low = (whole - high.astype(jnp.float32)).astype(jnp.bfloat16)
+    return jnp.stack([high, low])
+
+
+def twiddles(direction):
+    angle = direction * 2.0 * np.pi * (np.arange(INNER)[:, None] * np.arange(RADIX)[None, :]) / LENGTH
+    return np.stack([np.cos(angle), np.sin(angle)]).astype(np.float32)
+
+
+def butterflies(values, direction):
+    count = len(values)
+    if count == 1:
+        return values
+    even = butterflies(values[0::2], direction)
+    odd = butterflies(values[1::2], direction)
+    first, second = [], []
+    for k in range(count // 2):
+        (er, ei), (pr, pi) = even[k], odd[k]
+        if k == 0:
+            tr, ti = pr, pi
+        elif 4 * k == count:
+            tr, ti = (-pi, pr) if direction > 0 else (pi, -pr)
+        else:
+            c = math.cos(2.0 * math.pi * k / count)
+            d = direction * math.sin(2.0 * math.pi * k / count)
+            tr, ti = pr * c - pi * d, pr * d + pi * c
+        first.append((er + tr, ei + ti))
+        second.append((er - tr, ei - ti))
+    return first + second
+
+
+def halves(value):
+    high = value.astype(jnp.bfloat16)
+    return high, (value - high.astype(jnp.float32)).astype(jnp.bfloat16)
+
+
+def mul(a, b):
+    return jnp.dot(a, b, preferred_element_type=jnp.float32)
+
+
+def right_product(value, table):
+    high, low = halves(value)
+    return mul(low, table[0]) + mul(high, table[1]) + mul(high, table[0])
+
+
+def left_product(table, value):
+    high, low = halves(value)
+    return mul(table[1], high) + mul(table[0], low) + mul(table[0], high)
+
+
+def row_chunk(i):
+    return pl.ds(pl.multiple_of(i * 8, 8), 8)
+
+
+def forward_columns(field, table, twist, out, work):
+    rows = field.shape[1]
+
+    @pl.loop(0, rows // 8)
+    def _(i):
+        here = row_chunk(i)
+        values = [
+            (
+                field[0, here, a * RADIX : (a + 1) * RADIX],
+                field[1, here, a * RADIX : (a + 1) * RADIX],
+            )
+            for a in range(INNER)
+        ]
+        for c, (re, im) in enumerate(butterflies(values, -1.0)):
+            tr, ti = twist[0, c : c + 1, :], twist[1, c : c + 1, :]
+            work[c, here, :RADIX] = re * tr - im * ti
+            work[c, here, RADIX:] = re * ti + im * tr
+
+    @pl.loop(0, INNER)
+    def _(c):
+        out[c] = right_product(work[c], table)
+
+
+def move_rows(sense, data, factor, forward, backward, twist, out, work, spectrum):
+    @pl.loop(0, RADIX // 8)
+    def _(i):
+        here = row_chunk(i)
+        below = pl.ds(pl.multiple_of(RADIX + i * 8, 8), 8)
+        values = [(data[a, here, :RADIX], data[a, here, RADIX:]) for a in range(INNER)]
+        for c, (re, im) in enumerate(butterflies(values, -1.0)):
+            tr, ti = twist[0, c, here, :], twist[1, c, here, :]
+            side = slice((c % 2) * RADIX, (c % 2 + 1) * RADIX)
+            work[c // 2, here, side] = re * tr - im * ti
+            work[c // 2, below, side] = re * ti + im * tr
+
+    @pl.loop(0, INNER // 2)
+    def _(p):
+        spectrum[p] = left_product(forward, work[p])
+
+    for which in range(NREF):
+
+        @pl.loop(0, INNER // 2)
+        def _(p):
+            re, im = spectrum[p, :RADIX, :], spectrum[p, RADIX:, :]
+            fr, fi = factor[which, 0, p], sense * factor[which, 1, p]
+            moved = jnp.concatenate([re * fr - im * fi, re * fi + im * fr], axis=0)
+            work[p] = left_product(backward, moved)
+
+        @pl.loop(0, RADIX // 8)
+        def _(i):
+            here = row_chunk(i)
+            below = pl.ds(pl.multiple_of(RADIX + i * 8, 8), 8)
+            values = []
+            for c in range(INNER):
+                side = slice((c % 2) * RADIX, (c % 2 + 1) * RADIX)
+                re, im = work[c // 2, here, side], work[c // 2, below, side]
+                tr, ti = twist[0, c, here, :], twist[1, c, here, :]
+                values.append((re * tr + im * ti, im * tr - re * ti))
+            for a, (re, im) in enumerate(butterflies(values, 1.0)):
+                out[a, which, here, :RADIX] = re
+                out[a, which, here, RADIX:] = im
+
+
+def backward_columns(data, chosen, table, twist, out, work):
+    rows = data.shape[2]
+    for which in range(NREF):
+
+        @pl.loop(0, INNER)
+        def _(c):
+            work[c] = right_product(data[c, which], table)
+
+        @pl.loop(0, rows // 8)
+        def _(i):
+            here = row_chunk(i)
+            values = []
+            for c in range(INNER):
+                re, im = work[c, here, :RADIX], work[c, here, RADIX:]
+                tr, ti = twist[0, c : c + 1, :], twist[1, c : c + 1, :]
+                values.append((re * tr + im * ti, im * tr - re * ti))
+            for a, (re, im) in enumerate(butterflies(values, 1.0)):
+                side = slice(a * RADIX, (a + 1) * RADIX)
+                if which > 0:
+                    mine = chosen[here, side] == which
+                    re = jnp.where(mine, re, out[0, here, side])
+                    im = jnp.where(mine, im, out[1, here, side])
+                out[0, here, side] = re
+                out[1, here, side] = im
+
+
+def f32(*shape):
+    return jax.ShapeDtypeStruct(shape, jnp.float32)
+
+
+def cost(us_bytes):
+    return pl.CostEstimate(flops=2 * 10**9, bytes_accessed=us_bytes, transcendentals=0)
+
+
+def series(square, start):
+    total = jnp.full_like(square, (-1.0) ** 10 / math.factorial(20 + start))
+    for k in range(9, -1, -1):
+        total = total * square + (-1.0) ** k / math.factorial(2 * k + start)
+    return total
+
+
+def per_device(
+    source_field, rec_blocks, dest_device, dest_bin, slowness, ref_index, ref_slow, omega
+):
+    lanes = lax.axis_size("lat")
+    rows = source_field.shape[2]
+    columns = source_field.shape[3]
+    width = rec_blocks.shape[3]
+    fits = lanes == INNER and rows == RADIX and columns == LENGTH and width == RADIX
+    if not fits or rec_blocks.shape[2] != 1 or source_field.shape[1] != 1:
+        return general(
+            source_field, rec_blocks, dest_device, dest_bin, slowness, ref_index, ref_slow, omega
+        )
+    me = lax.axis_index("lat")
+    count = rec_blocks.shape[0]
+    per_row = columns // width
+    right_forward, right_backward = dft_tables(-1.0, False, 1.0), dft_tables(1.0, False, 1.0 / LENGTH)
+    left_forward, left_backward = dft_tables(-1.0, True, 1.0), dft_tables(1.0, True, 1.0 / LENGTH)
+    twist = jnp.asarray(twiddles(-1.0))
+    wide_twist = jnp.broadcast_to(twist[:, :, :, None], (2, INNER, RADIX, RADIX))
+    target = dest_device[:, 0] * (rows * per_row) + dest_bin
+    packed = jnp.concatenate(
+        [
+            rec_blocks.reshape(count, 2 * width),
+            jnp.broadcast_to(target.astype(jnp.float32)[:, None], (count, width)),
+        ],
+        axis=1,
+    )
+    packed = lax.all_gather(packed, "lat", axis=0, tiled=True)
+
+    spectrum = pl.pallas_call(
+        forward_columns,
+        out_shape=f32(INNER, rows, 2 * RADIX),
+        scratch_shapes=[pltpu.VMEM((INNER, rows, 2 * RADIX), jnp.float32)],
+        compiler_params=PARAMS,
+        cost_estimate=cost(2**23),
+        name="forward_columns",
+    )(source_field[:, 0], right_forward, twist)
+    source_part = lax.all_to_all(spectrum, "lat", split_axis=0, concat_axis=0, tiled=True)
+
+    step = 2.0 * math.pi / (LENGTH * SPACING) * DEPTH_STEP
+    number = jnp.arange(LENGTH, dtype=jnp.int32)
+    signed = jnp.where(number < LENGTH // 2, number, number - LENGTH).astype(jnp.float32) * step
+    squares = (signed * signed).reshape(RADIX, INNER)
+    kx_square = squares.T.reshape(INNER // 2, 2, RADIX).transpose(0, 2, 1)
+    ky_square = lax.dynamic_slice_in_dim(squares, me, 1, axis=1)[:, 0]
+    radial = (kx_square[:, :, :, None] + ky_square).reshape(INNER // 2, RADIX, 2 * RADIX)
+    limit = (omega[0] * ref_slow[0] * DEPTH_STEP) ** 2
+    argument = limit[:, None, None, None] - radial[None]
+    inside = jnp.maximum(argument, 0.0)
+    amplitude = jnp.exp(-jnp.sqrt(jnp.maximum(-argument, 0.0)))
+    factor = jnp.stack(
+        [
+            amplitude * series(inside, 0),
+            jnp.sign(omega[0]) * amplitude * jnp.sqrt(inside) * series(inside, 1),
+        ],
+        axis=1,
+    )
+
+    target = jnp.round(packed[:, 2 * width]).astype(jnp.int32)
+    row, place = target // per_row, target % per_row
+    own = lax.dynamic_slice_in_dim(twist, me, 1, axis=1)[:, 0]
+    turn = (place * me % INNER).astype(jnp.float32) * (-2.0 * math.pi / INNER)
+    turn_real, turn_imag = jnp.cos(turn)[:, None], jnp.sin(turn)[:, None]
+    weight_real = turn_real * own[0] - turn_imag * own[1]
+    weight_imag = turn_real * own[1] + turn_imag * own[0]
+    real, imag = packed[:, :width], packed[:, width : 2 * width]
+    turned = jnp.concatenate(
+        [real * weight_real - imag * weight_imag, real * weight_imag + imag * weight_real], axis=1
+    )
+    whole_table = right_forward[0].astype(jnp.float32) + right_forward[1].astype(jnp.float32)
+    traces = jnp.dot(turned, whole_table, precision=lax.Precision.HIGHEST)
+    spread = (jnp.arange(lanes * rows, dtype=jnp.int32)[:, None] == row[None, :]).astype(jnp.float32)
+    received_part = jnp.dot(spread, traces, precision=lax.Precision.HIGHEST)
+    received_part = received_part.reshape(INNER, RADIX, 2 * RADIX)
+
+    def propagate(part, sense, label):
+        moved = pl.pallas_call(
+            partial(move_rows, sense),
+            out_shape=f32(INNER, NREF, RADIX, 2 * RADIX),
+            scratch_shapes=[
+                pltpu.VMEM((INNER // 2, 2 * RADIX, 2 * RADIX), jnp.float32),
+                pltpu.VMEM((INNER // 2, 2 * RADIX, 2 * RADIX), jnp.float32),
+            ],
+            compiler_params=PARAMS,
+            cost_estimate=cost(2**25),
+            name="move_rows_" + label,
+        )(part, factor, left_forward, left_backward, wide_twist)
+        return lax.all_to_all(moved, "lat", split_axis=0, concat_axis=0, tiled=True)
+
+    chosen = ref_index[0]
+
+    def restore(back, label):
+        return pl.pallas_call(
+            backward_columns,
+            out_shape=f32(2, rows, columns),
+            scratch_shapes=[pltpu.VMEM((INNER, rows, 2 * RADIX), jnp.float32)],
+            compiler_params=PARAMS,
+            cost_estimate=cost(2**24),
+            name="backward_columns_" + label,
+        )(back, chosen, right_backward, twist)
+
+    received = restore(propagate(received_part, 1.0, "received"), "received")
+    source = restore(propagate(source_part, -1.0, "source"), "source")
+    speed = jnp.where(chosen == 1, ref_slow[0, 1], ref_slow[0, 0])
+    double = (2.0 * DEPTH_STEP) * omega[0] * (slowness[0] - speed)
+    square = double * double
+    cosine, sine = series(square, 0), double * series(square, 1)
+    cross_real = source[0] * received[0] + source[1] * received[1]
+    cross_imag = source[1] * received[0] - source[0] * received[1]
+    return (cross_real * cosine + cross_imag * sine)[None]
+
+
 def solution(mesh):
     return jax.shard_map(
         per_device,

time: 523 us -> 312 us (0.60)
  matrix products: 164 us -> 1.89 us
  local copies, waits for them, and re-layouts: 73.2 us -> 10.8 us
  Pallas kernels: 0 us -> 55.9 us
  blocking collectives: 0 us -> 52.2 us
  waiting for transfers between devices: 210 us -> 160 us
  starting transfers between devices: 39.9 us -> 16.6 us
  other arithmetic: 28 us -> 13.1 us
    dot_general x42 -> x3, matrix products: 164 us -> 1.89 us  [the longest x1 1.06 us: per_device(): received_part = jnp.dot(spread, traces, precision=lax.Precision.HIGHEST)]
    pallas_call x0 -> x5, Pallas kernels: none -> 55.9 us  [the longest x2 28.7 us: propagate(): pl.pallas_call(partial(move_rows, sense), out_shape=f32(INNER, NREF, RADI...]
    all_gather x0 -> x1, blocking collectives: none -> 52.2 us  [per_device(): packed = lax.all_gather(packed, 'lat', axis=0, tiled=True)]
    all_to_all x7 -> x3, waiting for transfers between devices: 210 us -> 160 us  [the longest x2 160 us: propagate(): return lax.all_to_all(moved, 'lat', split_axis=0, concat_axis=0, tiled=True)]
    reshape x6 -> x0, local copies, waits for them, and re-layouts: 27 us -> none  [the longest x4 27 us: transform(): return (work_real.reshape(initial), work_imag.reshape(initial))]
    another operation x2 -> x0, local copies, waits for them, and re-layouts: 24.5 us -> none  [the longest x1 12.3 us: per_device(): stacked_imag = jnp.stack(shifted_imag, axis=1)]
    all_to_all x7 -> x3, starting transfers between devices: 39.9 us -> 16.6 us  [the longest x2 9.96 us: propagate(): return lax.all_to_all(moved, 'lat', split_axis=0, concat_axis=0, tiled=True)]
    select_n x1, other arithmetic: 18.7 us -> 0.01 us  [per_device(): row, place = (target // per_row, target % per_row)]
  transfers between devices with their start and end apart: 7 -> 3, of which waited for: 5 -> 2; matrix products, arithmetic and copies ran while one was open for 20% -> 6% of each run, Pallas kernels for 0% -> 13%
where the time goes in v1:
time: 312 us; the launch traced here: 311 us
  waiting for transfers between devices  160 us (51%)
  Pallas kernels  55.9 us (18%)
  blocking collectives  52.2 us (17%)
  starting transfers between devices  16.6 us (5%)
  other arithmetic  13.1 us (4%)
  local copies, waits for them, and re-layouts  10.8 us (3%)
    all_to_all x2, waiting for transfers between devices, propagate(): return lax.all_to_all(moved, 'lat', split_axis=0, concat_axis=0, tiled=True)  160 us
    all_gather x1, blocking collectives, per_device(): packed = lax.all_gather(packed, 'lat', axis=0, tiled=True)  52.2 us
    pallas_call x2, Pallas kernels, propagate(): pl.pallas_call(partial(move_rows, sense), out_shape=f32(INNER, NREF, RADI...  28.7 us
    pallas_call x2, Pallas kernels, restore(): pl.pallas_call(backward_columns, out_shape=f32(2, rows, columns), scratch...  21.4 us
    all_to_all x2, starting transfers between devices, propagate(): return lax.all_to_all(moved, 'lat', split_axis=0, concat_axis=0, tiled=True)  9.96 us
    all_to_all x1, starting transfers between devices, per_device(): lax.all_to_all(spectrum, 'lat', split_axis=0, concat_axis=0, tiled=True)  6.69 us
  transfers between devices with their start and end apart: 3, of which 2 were waited for; matrix products, arithmetic and copies ran while one was open for 6% of the time, Pallas kernels for 13%

profile of v1, /device:TPU:11, one launch (start us, length us, event | category | flops | bytes accessed | tf_op | source)
XLA Modules:
  0.0 311.0 jit_solution(4367601782724953569)
XLA Ops:
  0.0 0.7 copy-done.5
  0.7 0.9 copy-done.7
  1.7 5.8 %forward_columns.1 = f32[16,128,256]{2,1,0:T(8,128)S(1)} custom-call(f32[2,128,2048]{2,1,0:T(8,128)} %bitcast.37, bf16[2,256,256]{2,1,0:T(8,128)(2,1)S(1)} %copy-done.7, f32[2,16,128]{2,1,0:T(8,128)S(1)} %copy-done.5), custom_call_target="tpu_custom_call" | custom-call | flops 2000000000 | bytes 8388608 | tf_op jit(solution)/shard_map/forward_columns/pallas_call | solution.py:382
  7.4 1.3 copy-done.1
  8.8 6.7 %all-to-all-start = ((f32[16,128,256]{2,1,0:T(8,128)}), f32[16,128,256]{2,1,0:T(8,128)S(1)}, u32[]{:S(2)}, u32[]{:S(2)}) async-start(f32[16,128,256]{2,1,0:T(8,128)} %copy-done.1), calls=%async_computation | async-start | bytes 4194304 | tf_op jit(solution)/shard_map/all_to_all | solution.py:390
  15.6 1.0 copy.15
  16.6 2.2 add.471
  18.9 1.8 add.472
  21.5 52.2 %all_gather.3 = f32[256,384]{1,0:T(8,128)S(1)} all-gather(f32[16,384]{1,0:T(8,128)S(1)} %pad_maximum_fusion.1), channel_id=1, replica_groups=mesh['shots'=2,'lat'=16] {'lat'}, dimensions={0}, use_global_device_ids=true | all-gather | bytes 417792 | tf_op jit(solution)/shard_map/all_gather | solution.py:380
  73.8 0.7 cosine_reduce_fusion
  74.5 1.3 broadcast_add_fusion
  75.8 4.4 %fusion.31 = (f32[2,1,8,128,256]{4,3,2,1,0:T(8,128)S(1)}, f32[2,1,8,128,256]{4,3,2,1,0:T(8,128)S(1)}) fusion(f32[8,128,256]{2,1,0:T(8,128)S(1)} %broadcast_add_fusion, f32[2]{0:T(128)S(1)} %multiply_bitcast_fusion.1, f32[]{:T(128)S(6)} %sign.13), kind=kLoop, calls=%fused_computation.34 | loop fusion | flops 25690112 | bytes 5242892 | tf_op jit(solution)/shard_map/mul | solution.py:405
  80.2 2.3 pad_maximum_fusion.factor
  83.4 1.1 fusion.49
  84.5 1.9 broadcast_in_dim.22.twist
  86.4 14.3 %move_rows_received.1 = f32[16,2,128,256]{3,2,1,0:T(8,128)} custom-call(f32[16,128,256]{2,1,0:T(8,128)S(1)} %bitcast.34, f32[2,2,8,128,256]{4,3,2,1,0:T(8,128)} %pad_maximum_fusion.factor, bf16[2,256,256]{2,1,0:T(8,128)(2,1)S(1)} %copy-done.2, bf16[2,256,256]{2,1,0:T(8,128)(2,1)S(1)} %copy-done.3, f32[2,16,128,128]{3,2,1,0:T(8,128)} %broadcast_in_dim.22.twist), custom_call_target="tpu_custom_call" | custom-call | flops 2000000000 | bytes 33554432 | tf_op jit(solution)/shard_map/move_rows_received/pallas_call | solution.py:429
  100.7 5.0 %all-to-all-start.2 = ((f32[16,2,128,256]{3,2,1,0:T(8,128)}), f32[16,2,128,256]{3,2,1,0:T(8,128)}, u32[]{:S(2)}, u32[]{:S(2)}) async-start(f32[16,2,128,256]{3,2,1,0:T(8,128)} %move_rows_received.1), calls=%async_computation.2 | async-start | bytes 8388608 | tf_op jit(solution)/shard_map/all_to_all | solution.py:440
  105.7 14.5 %move_rows_source.1 = f32[16,2,128,256]{3,2,1,0:T(8,128)} custom-call(f32[16,128,256]{2,1,0:T(8,128)S(1)} %all-to-all-done.data, f32[2,2,8,128,256]{4,3,2,1,0:T(8,128)} %pad_maximum_fusion.factor, bf16[2,256,256]{2,1,0:T(8,128)(2,1)S(1)} %copy-done.2, bf16[2,256,256]{2,1,0:T(8,128)(2,1)S(1)} %copy-done.3, f32[2,16,128,128]{3,2,1,0:T(8,128)} %broadcast_in_dim.22.twist), custom_call_target="tpu_custom_call" | custom-call | flops 2000000000 | bytes 33554432 | tf_op jit(solution)/shard_map/move_rows_source/pallas_call | solution.py:429
  120.1 78.5 %all-to-all-done.2.data = f32[16,2,128,256]{3,2,1,0:T(8,128)} async-done(((f32[16,2,128,256]{3,2,1,0:T(8,128)}), f32[16,2,128,256]{3,2,1,0:T(8,128)}, u32[]{:S(2)}, u32[]{:S(2)}) %all-to-all-start.2) | async-done | bytes 4194336 | tf_op jit(solution)/shard_map/all_to_all | solution.py:440
  198.6 5.0 %all-to-all-start.1 = ((f32[16,2,128,256]{3,2,1,0:T(8,128)}), f32[16,2,128,256]{3,2,1,0:T(8,128)}, u32[]{:S(2)}, u32[]{:S(2)}) async-start(f32[16,2,128,256]{3,2,1,0:T(8,128)} %move_rows_source.1), calls=%async_computation.1 | async-start | bytes 8388608 | tf_op jit(solution)/shard_map/all_to_all | solution.py:440
  204.3 10.7 %backward_columns_received.1 = f32[2,128,2048]{2,1,0:T(8,128)S(1)} custom-call(f32[16,2,128,256]{3,2,1,0:T(8,128)} %all-to-all-done.2.data, s32[128,2048]{1,0:T(8,128)S(1)} %bitcast.32, bf16[2,256,256]{2,1,0:T(8,128)(2,1)S(1)} %copy-done.4, f32[2,16,128]{2,1,0:T(8,128)S(1)} %copy-done.6), custom_call_target="tpu_custom_call" | custom-call | flops 2000000000 | bytes 16777216 | tf_op jit(solution)/shard_map/backward_columns_received/pallas_call | solution.py:445
  215.0 81.1 %all-to-all-done.1.data = f32[16,2,128,256]{3,2,1,0:T(8,128)} async-done(((f32[16,2,128,256]{3,2,1,0:T(8,128)}), f32[16,2,128,256]{3,2,1,0:T(8,128)}, u32[]{:S(2)}, u32[]{:S(2)}) %all-to-all-start.1) | async-done | bytes 4194336 | tf_op jit(solution)/shard_map/all_to_all | solution.py:440
  296.1 10.8 %backward_columns_source.1 = f32[2,128,2048]{2,1,0:T(8,128)S(1)} custom-call(f32[16,2,128,256]{3,2,1,0:T(8,128)} %all-to-all-done.1.data, s32[128,2048]{1,0:T(8,128)S(1)} %bitcast.33, bf16[2,256,256]{2,1,0:T(8,128)(2,1)S(1)} %copy-done.4, f32[2,16,128]{2,1,0:T(8,128)S(1)} %copy-done.6), custom_call_target="tpu_custom_call" | custom-call | flops 2000000000 | bytes 16777216 | tf_op jit(solution)/shard_map/backward_columns_source/pallas_call | solution.py:445
  306.9 4.2 %multiply_add_fusion = f32[1,128,2048]{2,1,0:T(8,128)} fusion(f32[1,128,2048]{2,1,0:T(8,128)S(1)} %copy-done.8, f32[2,128,2048]{2,1,0:T(8,128)S(1)} %backward_columns_received.1, f32[2,128,2048]{2,1,0:T(8,128)S(1)} %backward_columns_source.1, s32[1,128,2048]{2,1,0:T(8,128)S(1)} %copy-done, f32[]{:T(128)} %bitcast.11, f32[]{:T(128)} %bitcast.10, ...), kind=kLoop, calls=%fused_computation.55 | loop fusion | flops 14417920 | bytes 7340044 | tf_op jit(solution)/shard_map/add | solution.py:462
  (44 shorter events, 1.9 us)
Async XLA Ops:
  0.0 0.7 copy-start.5
  0.7 0.9 copy-start.7
  7.4 1.3 copy-start.1
  8.8 6.8 %copy-start.11 = (f32[16,2,1,128]{3,2,1,0:T(1,128)S(1)}, f32[16,2,1,128]{3,2,1,0:T(1,128)}, u32[]{:S(2)}) copy-start(f32[16,2,1,128]{3,2,1,0:T(1,128)} %param.14) | copy-start | bytes 49156
  8.8 91.9 %all-to-all-start = ((f32[16,128,256]{2,1,0:T(8,128)}), f32[16,128,256]{2,1,0:T(8,128)S(1)}, u32[]{:S(2)}, u32[]{:S(2)}) async-start(f32[16,128,256]{2,1,0:T(8,128)} %copy-done.1), calls=%async_computation | async-start | bytes 4194304 | tf_op jit(solution)/shard_map/all_to_all | solution.py:390
  15.6 5.8 %copy-start.6 = (f32[2,16,128]{2,1,0:T(8,128)S(1)}, f32[2,16,128]{2,1,0:T(8,128)}, u32[]{:S(2)}) copy-start(f32[2,16,128]{2,1,0:T(8,128)} %constant.138.clone.twist) | copy-start | bytes 49156
  15.6 5.8 %copy-start.13 = (s32[16]{0:T(128)S(1)}, s32[16]{0:T(128)}, u32[]{:S(2)}) copy-start(s32[16]{0:T(128)} %param.16) | copy-start | bytes 196
  15.6 5.8 %copy-start.14 = (s32[16,1]{0,1:T(1,128)S(1)}, s32[16,1]{0,1:T(1,128)}, u32[]{:S(2)}) copy-start(s32[16,1]{0,1:T(1,128)} %param.15) | copy-start | bytes 196
  16.6 57.8 %copy-start.12 = (f32[1,2]{1,0:T(1,128)S(1)}, f32[1,2]{1,0:T(1,128)}, u32[]{:S(2)}) copy-start(f32[1,2]{1,0:T(1,128)} %param.19) | copy-start | bytes 28
  80.2 2.4 copy-start.10
  80.2 2.8 copy-start.9
  83.4 3.0 copy-start.2
  83.4 3.0 copy-start.3
  100.7 97.9 %all-to-all-start.2 = ((f32[16,2,128,256]{3,2,1,0:T(8,128)}), f32[16,2,128,256]{3,2,1,0:T(8,128)}, u32[]{:S(2)}, u32[]{:S(2)}) async-start(f32[16,2,128,256]{3,2,1,0:T(8,128)} %move_rows_received.1), calls=%async_computation.2 | async-start | bytes 8388608 | tf_op jit(solution)/shard_map/all_to_all | solution.py:440
  120.1 84.1 %copy-start = (s32[1,128,2048]{2,1,0:T(8,128)S(1)}, s32[1,128,2048]{2,1,0:T(8,128)}, u32[]{:S(2)}) copy-start(s32[1,128,2048]{2,1,0:T(8,128)} %param.18) | copy-start | bytes 3145732
  120.1 84.1 %copy-start.4 = (bf16[2,256,256]{2,1,0:T(8,128)(2,1)S(1)}, bf16[2,256,256]{2,1,0:T(8,128)(2,1)}, u32[]{:S(2)}) copy-start(bf16[2,256,256]{2,1,0:T(8,128)(2,1)} %constant.170.table) | copy-start | bytes 786436
  198.6 97.5 %all-to-all-start.1 = ((f32[16,2,128,256]{3,2,1,0:T(8,128)}), f32[16,2,128,256]{3,2,1,0:T(8,128)}, u32[]{:S(2)}, u32[]{:S(2)}) async-start(f32[16,2,128,256]{3,2,1,0:T(8,128)} %move_rows_source.1), calls=%async_computation.1 | async-start | bytes 8388608 | tf_op jit(solution)/shard_map/all_to_all | solution.py:440
  296.1 10.8 %copy-start.8 = (f32[1,128,2048]{2,1,0:T(8,128)S(1)}, f32[1,128,2048]{2,1,0:T(8,128)}, u32[]{:S(2)}) copy-start(f32[1,128,2048]{2,1,0:T(8,128)} %param.17) | copy-start | bytes 3145732

commit v2 on v1

--- a/solution.py
+++ b/solution.py
@@ -309,13 +309,12 @@
                 out[a, which, here, RADIX:] = im
 
 
-def backward_columns(data, chosen, table, twist, out, work):
+def backward_columns(data, chosen, table, twist, *rest):
+    other, out, work, keep = rest if len(rest) == 4 else (None, *rest)
     rows = data.shape[2]
     for which in range(NREF):
-
-        @pl.loop(0, INNER)
-        def _(c):
-            work[c] = right_product(data[c, which], table)
+        flat = data[:, which].reshape(INNER * rows, 2 * RADIX)
+        work[...] = right_product(flat, table).reshape(INNER, rows, 2 * RADIX)
 
         @pl.loop(0, rows // 8)
         def _(i):
@@ -329,10 +328,16 @@
                 side = slice(a * RADIX, (a + 1) * RADIX)
                 if which > 0:
                     mine = chosen[here, side] == which
-                    re = jnp.where(mine, re, out[0, here, side])
-                    im = jnp.where(mine, im, out[1, here, side])
-                out[0, here, side] = re
-                out[1, here, side] = im
+                    re = jnp.where(mine, re, keep[0, here, side])
+                    im = jnp.where(mine, im, keep[1, here, side])
+                if which < NREF - 1:
+                    keep[0, here, side] = re
+                    keep[1, here, side] = im
+                elif other is None:
+                    out[0, here, side] = re
+                    out[1, here, side] = im
+                else:
+                    out[here, side] = other[0, here, side] * re + other[1, here, side] * im
 
 
 def f32(*shape):
@@ -377,8 +382,6 @@
         ],
         axis=1,
     )
-    packed = lax.all_gather(packed, "lat", axis=0, tiled=True)
-
     spectrum = pl.pallas_call(
         forward_columns,
         out_shape=f32(INNER, rows, 2 * RADIX),
@@ -388,6 +391,10 @@
         name="forward_columns",
     )(source_field[:, 0], right_forward, twist)
     source_part = lax.all_to_all(spectrum, "lat", split_axis=0, concat_axis=0, tiled=True)
+    packed, source_part = lax.optimization_barrier((packed, source_part))
+    copies = jnp.broadcast_to(packed[None], (lanes,) + packed.shape)
+    packed = lax.all_to_all(copies, "lat", split_axis=0, concat_axis=0, tiled=True)
+    packed = packed.reshape(lanes * count, 3 * width)
 
     step = 2.0 * math.pi / (LENGTH * SPACING) * DEPTH_STEP
     number = jnp.arange(LENGTH, dtype=jnp.int32)
@@ -408,6 +415,25 @@
         axis=1,
     )
 
+    def propagate(part, sense, label):
+        return pl.pallas_call(
+            partial(move_rows, sense),
+            out_shape=f32(INNER, NREF, RADIX, 2 * RADIX),
+            scratch_shapes=[
+                pltpu.VMEM((INNER // 2, 2 * RADIX, 2 * RADIX), jnp.float32),
+                pltpu.VMEM((INNER // 2, 2 * RADIX, 2 * RADIX), jnp.float32),
+            ],
+            compiler_params=PARAMS,
+            cost_estimate=cost(2**25),
+            name="move_rows_" + label,
+        )(part, factor, left_forward, left_backward, wide_twist)
+
+    def send_back(moved):
+        return lax.all_to_all(moved, "lat", split_axis=0, concat_axis=0, tiled=True)
+
+    packed, moved = lax.optimization_barrier((packed, propagate(source_part, -1.0, "source")))
+    source_back = send_back(moved)
+
     target = jnp.round(packed[:, 2 * width]).astype(jnp.int32)
     row, place = target // per_row, target % per_row
     own = lax.dynamic_slice_in_dim(twist, me, 1, axis=1)[:, 0]
@@ -425,41 +451,44 @@
     received_part = jnp.dot(spread, traces, precision=lax.Precision.HIGHEST)
     received_part = received_part.reshape(INNER, RADIX, 2 * RADIX)
 
-    def propagate(part, sense, label):
-        moved = pl.pallas_call(
-            partial(move_rows, sense),
-            out_shape=f32(INNER, NREF, RADIX, 2 * RADIX),
-            scratch_shapes=[
-                pltpu.VMEM((INNER // 2, 2 * RADIX, 2 * RADIX), jnp.float32),
-                pltpu.VMEM((INNER // 2, 2 * RADIX, 2 * RADIX), jnp.float32),
-            ],
-            compiler_params=PARAMS,
-            cost_estimate=cost(2**25),
-            name="move_rows_" + label,
-        )(part, factor, left_forward, left_backward, wide_twist)
-        return lax.all_to_all(moved, "lat", split_axis=0, concat_axis=0, tiled=True)
-
     chosen = ref_index[0]
 
-    def restore(back, label):
+    share = rows // 4
+
+    def restore(back, label, *other):
+        fields = pl.BlockSpec((2, share, columns), lambda i: (0, i, 0))
+        plane = pl.BlockSpec((share, columns), lambda i: (i, 0))
         return pl.pallas_call(
             backward_columns,
-            out_shape=f32(2, rows, columns),
-            scratch_shapes=[pltpu.VMEM((INNER, rows, 2 * RADIX), jnp.float32)],
+            grid=(rows // share,),
+            in_specs=[
+                pl.BlockSpec((INNER, NREF, share, 2 * RADIX), lambda i: (0, 0, i, 0)),
+                plane,
+                pl.BlockSpec((2, 2 * RADIX, 2 * RADIX), lambda i: (0, 0, 0)),
+                pl.BlockSpec((2, INNER, RADIX), lambda i: (0, 0, 0)),
+            ]
+            + [fields] * len(other),
+            out_specs=plane if other else fields,
+            out_shape=f32(rows, columns) if other else f32(2, rows, columns),
+            scratch_shapes=[
+                pltpu.VMEM((INNER, share, 2 * RADIX), jnp.float32),
+                pltpu.VMEM((2, share, columns), jnp.float32),
+            ],
             compiler_params=PARAMS,
             cost_estimate=cost(2**24),
             name="backward_columns_" + label,
-        )(back, chosen, right_backward, twist)
-
-    received = restore(propagate(received_part, 1.0, "received"), "received")
-    source = restore(propagate(source_part, -1.0, "source"), "source")
+        )(back, chosen, right_backward, twist, *other)
+
+    received_back = send_back(propagate(received_part, 1.0, "received"))
+    source = restore(source_back, "source")
     speed = jnp.where(chosen == 1, ref_slow[0, 1], ref_slow[0, 0])
     double = (2.0 * DEPTH_STEP) * omega[0] * (slowness[0] - speed)
     square = double * double
     cosine, sine = series(square, 0), double * series(square, 1)
-    cross_real = source[0] * received[0] + source[1] * received[1]
-    cross_imag = source[1] * received[0] - source[0] * received[1]
-    return (cross_real * cosine + cross_imag * sine)[None]
+    turned_source = jnp.stack(
+        [source[0] * cosine + source[1] * sine, source[1] * cosine - source[0] * sine]
+    )
+    return restore(received_back, "image", turned_source)[None]
 
 
 def solution(mesh):

time: 312 us -> 297 us (0.952)
  blocking collectives: 52.2 us -> 0 us
  waiting for transfers between devices: 160 us -> 197 us
  starting transfers between devices: 16.6 us -> 22.7 us
  Pallas kernels: 55.9 us -> 50.2 us
    all_gather x1 -> x0, blocking collectives: 52.2 us -> none  [per_device(): packed = lax.all_gather(packed, 'lat', axis=0, tiled=True)]
    all_to_all x1, waiting for transfers between devices: 0.01 us -> 40.1 us  [per_device(): lax.all_to_all(spectrum, 'lat', split_axis=0, concat_axis=0, tiled=True)]
    all_to_all x2 -> x3, starting transfers between devices: 9.96 us -> 16 us  [the longest x2 11.1 us: send_back(): return lax.all_to_all(moved, 'lat', split_axis=0, concat_axis=0, tiled=True)]
    pallas_call x2, Pallas kernels: 21.4 us -> 15.7 us  [restore(): pl.pallas_call(backward_columns, grid=(rows // share,), in_specs=[pl.Bloc...]
    all_to_all x2 -> x3, waiting for transfers between devices: 160 us -> 156 us  [the longest x2 156 us: send_back(): return lax.all_to_all(moved, 'lat', split_axis=0, concat_axis=0, tiled=True)]
  transfers between devices with their start and end apart: 3 -> 4, of which waited for: 2 -> 3; matrix products, arithmetic and copies ran while one was open for 6% -> 7% of each run, Pallas kernels for 13% -> 12%
where the time goes in v2:
time: 297 us; the launch traced here: 296 us
  waiting for transfers between devices  197 us (66%)
  Pallas kernels  50.2 us (17%)
  starting transfers between devices  22.7 us (8%)
  other arithmetic  12.2 us (4%)
  local copies, waits for them, and re-layouts  11.5 us (4%)
    all_to_all x2, waiting for transfers between devices, send_back(): return lax.all_to_all(moved, 'lat', split_axis=0, concat_axis=0, tiled=True)  156 us
    all_to_all x1, waiting for transfers between devices, per_device(): lax.all_to_all(spectrum, 'lat', split_axis=0, concat_axis=0, tiled=True)  40.1 us
    pallas_call x2, Pallas kernels, propagate(): pl.pallas_call(partial(move_rows, sense), out_shape=f32(INNER, NREF, RADI...  28.7 us
    pallas_call x2, Pallas kernels, restore(): pl.pallas_call(backward_columns, grid=(rows // share,), in_specs=[pl.Bloc...  15.7 us
    all_to_all x2, starting transfers between devices, send_back(): return lax.all_to_all(moved, 'lat', split_axis=0, concat_axis=0, tiled=True)  11.1 us
    all_to_all x1, starting transfers between devices, per_device(): lax.all_to_all(spectrum, 'lat', split_axis=0, concat_axis=0, tiled=True)  6.69 us
  transfers between devices with their start and end apart: 4, of which 3 were waited for; matrix products, arithmetic and copies ran while one was open for 7% of the time, Pallas kernels for 12%

profile of v2, /device:TPU:11, one launch (start us, length us, event | category | flops | bytes accessed | tf_op | source)
XLA Modules:
  0.0 295.8 jit_solution(35857319265292633)
XLA Ops:
  0.7 0.9 copy-done.7
  1.7 5.8 %forward_columns.1 = f32[16,128,256]{2,1,0:T(8,128)S(1)} custom-call(f32[2,128,2048]{2,1,0:T(8,128)} %bitcast.43, bf16[2,256,256]{2,1,0:T(8,128)(2,1)S(1)} %copy-done.7, f32[2,16,128]{2,1,0:T(8,128)S(1)} %copy-done.5), custom_call_target="tpu_custom_call" | custom-call | flops 2000000000 | bytes 8388608 | tf_op jit(solution)/shard_map/forward_columns/pallas_call | solution.py:385
  7.4 1.3 copy-done.1
  8.8 6.7 %all-to-all-start = ((f32[16,128,256]{2,1,0:T(8,128)}), f32[16,128,256]{2,1,0:T(8,128)S(1)}, u32[]{:S(2)}, u32[]{:S(2)}) async-start(f32[16,128,256]{2,1,0:T(8,128)} %copy-done.1), calls=%async_computation | async-start | bytes 4194304 | tf_op jit(solution)/shard_map/all_to_all | solution.py:393
  16.3 1.0 copy.15
  17.3 2.2 add.488
  19.5 1.8 add.489
  21.4 1.3 broadcast_add_fusion
  22.8 40.1 %all-to-all-done.data = f32[16,128,256]{2,1,0:T(8,128)S(1)} async-done(((f32[16,128,256]{2,1,0:T(8,128)}), f32[16,128,256]{2,1,0:T(8,128)S(1)}, u32[]{:S(2)}, u32[]{:S(2)}) %all-to-all-start) | async-done | bytes 2097184 | tf_op jit(solution)/shard_map/all_to_all | solution.py:393
  62.9 0.8 broadcast_in_dim.23
  63.7 4.9 %all-to-all-start.1 = ((f32[16,16,384]{2,1,0:T(8,128)}), f32[16,16,384]{2,1,0:T(8,128)S(1)}, u32[]{:S(2)}, u32[]{:S(2)}) async-start(f32[16,16,384]{2,1,0:T(8,128)} %broadcast_in_dim.23), calls=%async_computation.1 | async-start | bytes 786432 | tf_op jit(solution)/shard_map/all_to_all | solution.py:396
  68.6 4.4 %fusion.31 = (f32[2,1,8,128,256]{4,3,2,1,0:T(8,128)S(1)}, f32[2,1,8,128,256]{4,3,2,1,0:T(8,128)S(1)}) fusion(f32[8,128,256]{2,1,0:T(8,128)S(1)} %broadcast_add_fusion, f32[2]{0:T(128)S(1)} %multiply_bitcast_fusion.1, f32[]{:T(128)S(6)} %sign.13), kind=kLoop, calls=%fused_computation.34 | loop fusion | flops 25690112 | bytes 5242892 | tf_op jit(solution)/shard_map/mul | solution.py:412
  73.0 2.3 pad_maximum_fusion.factor
  75.3 1.9 broadcast_in_dim.51.twist
  77.2 14.4 %move_rows_source.1 = f32[16,2,128,256]{3,2,1,0:T(8,128)} custom-call(f32[16,128,256]{2,1,0:T(8,128)S(1)} %all-to-all-done.data, f32[2,2,8,128,256]{4,3,2,1,0:T(8,128)} %pad_maximum_fusion.factor, bf16[2,256,256]{2,1,0:T(8,128)(2,1)S(1)} %copy-done.3, bf16[2,256,256]{2,1,0:T(8,128)(2,1)S(1)} %copy-done.2, f32[2,16,128,128]{3,2,1,0:T(8,128)} %broadcast_in_dim.51.twist), custom_call_target="tpu_custom_call" | custom-call | flops 2000000000 | bytes 33554432 | tf_op jit(solution)/shard_map/move_rows_source/pallas_call | solution.py:419
  91.7 6.2 %all-to-all-start.3 = ((f32[16,2,128,256]{3,2,1,0:T(8,128)}), f32[16,2,128,256]{3,2,1,0:T(8,128)}, u32[]{:S(2)}, u32[]{:S(2)}) async-start(f32[16,2,128,256]{3,2,1,0:T(8,128)} %move_rows_source.1), calls=%async_computation.3 | async-start | bytes 8388608 | tf_op jit(solution)/shard_map/all_to_all | solution.py:432
  99.5 1.1 fusion.49
  100.6 14.3 %move_rows_received.1 = f32[16,2,128,256]{3,2,1,0:T(8,128)} custom-call(f32[16,128,256]{2,1,0:T(8,128)S(1)} %bitcast.36, f32[2,2,8,128,256]{4,3,2,1,0:T(8,128)} %pad_maximum_fusion.factor, bf16[2,256,256]{2,1,0:T(8,128)(2,1)S(1)} %copy-done.3, bf16[2,256,256]{2,1,0:T(8,128)(2,1)S(1)} %copy-done.2, f32[2,16,128,128]{3,2,1,0:T(8,128)} %broadcast_in_dim.51.twist), custom_call_target="tpu_custom_call" | custom-call | flops 2000000000 | bytes 33554432 | tf_op jit(solution)/shard_map/move_rows_received/pallas_call | solution.py:419
  114.9 75.4 %all-to-all-done.3.data = f32[16,2,128,256]{3,2,1,0:T(8,128)} async-done(((f32[16,2,128,256]{3,2,1,0:T(8,128)}), f32[16,2,128,256]{3,2,1,0:T(8,128)}, u32[]{:S(2)}, u32[]{:S(2)}) %all-to-all-start.3) | async-done | bytes 4194336 | tf_op jit(solution)/shard_map/all_to_all | solution.py:432
  190.3 4.9 %all-to-all-start.2 = ((f32[16,2,128,256]{3,2,1,0:T(8,128)}), f32[16,2,128,256]{3,2,1,0:T(8,128)}, u32[]{:S(2)}, u32[]{:S(2)}) async-start(f32[16,2,128,256]{3,2,1,0:T(8,128)} %move_rows_received.1), calls=%async_computation.2 | async-start | bytes 8388608 | tf_op jit(solution)/shard_map/all_to_all | solution.py:432
  195.8 7.5 %backward_columns_source.1 = f32[2,128,2048]{2,1,0:T(8,128)S(1)} custom-call(f32[16,2,128,256]{3,2,1,0:T(8,128)} %all-to-all-done.3.data, s32[128,2048]{1,0:T(8,128)S(1)} %bitcast.34, bf16[2,256,256]{2,1,0:T(8,128)(2,1)S(1)} %copy-done.4, f32[2,16,128]{2,1,0:T(8,128)S(1)} %copy-done.6), custom_call_target="tpu_custom_call" | custom-call | flops 2000000000 | bytes 16777216 | tf_op jit(solution)/shard_map/backward_columns_source/pallas_call | solution.py:461
  203.4 3.0 %multiply_add_fusion = (f32[1,128,2048]{2,1,0:T(8,128)S(1)}, f32[1,128,2048]{2,1,0:T(8,128)S(1)}) fusion(f32[2,128,2048]{2,1,0:T(8,128)S(1)} %backward_columns_source.1, f32[1,128,2048]{2,1,0:T(8,128)S(1)} %copy-done.8, f32[]{:T(128)} %bitcast.12, f32[]{:T(128)} %bitcast.11, s32[1,128,2048]{2,1,0:T(8,128)S(1)} %copy-done, f32[]{:T(128)S(6)} %mul_shard_map.3), kind=kLoop, calls=%fused_computation.57 | loop fusion | flops 13631488 | bytes 6291468 | tf_op jit(solution)/shard_map/add | solution.py:489
  206.6 81.1 %all-to-all-done.2.data = f32[16,2,128,256]{3,2,1,0:T(8,128)} async-done(((f32[16,2,128,256]{3,2,1,0:T(8,128)}), f32[16,2,128,256]{3,2,1,0:T(8,128)}, u32[]{:S(2)}, u32[]{:S(2)}) %all-to-all-start.2) | async-done | bytes 4194336 | tf_op jit(solution)/shard_map/all_to_all | solution.py:432
  287.7 8.2 %backward_columns_image.1 = f32[128,2048]{1,0:T(8,128)} custom-call(f32[16,2,128,256]{3,2,1,0:T(8,128)} %all-to-all-done.2.data, s32[128,2048]{1,0:T(8,128)S(1)} %bitcast.35, bf16[2,256,256]{2,1,0:T(8,128)(2,1)S(1)} %copy-done.4, f32[2,16,128]{2,1,0:T(8,128)S(1)} %copy-done.6, f32[2,128,2048]{2,1,0:T(8,128)S(1)} %pad_maximum_fusion.1.rest_0_), custom_call_target="tpu_custom_call" | custom-call | flops 2000000000 | bytes 16777216 | tf_op jit(solution)/shard_map/backward_columns_image/pallas_call | solution.py:461
  (49 shorter events, 3.4 us)
Async XLA Ops:
  0.0 0.7 copy-start.5
  0.7 0.9 copy-start.7
  7.4 1.3 copy-start.1
  8.8 7.3 %copy-start.11 = (f32[16,2,1,128]{3,2,1,0:T(1,128)S(1)}, f32[16,2,1,128]{3,2,1,0:T(1,128)}, u32[]{:S(2)}) copy-start(f32[16,2,1,128]{3,2,1,0:T(1,128)} %param.14) | copy-start | bytes 49156
  8.8 54.1 %all-to-all-start = ((f32[16,128,256]{2,1,0:T(8,128)}), f32[16,128,256]{2,1,0:T(8,128)S(1)}, u32[]{:S(2)}, u32[]{:S(2)}) async-start(f32[16,128,256]{2,1,0:T(8,128)} %copy-done.1), calls=%async_computation | async-start | bytes 4194304 | tf_op jit(solution)/shard_map/all_to_all | solution.py:393
  16.2 5.1 %copy-start.14 = (s32[16]{0:T(128)S(1)}, s32[16]{0:T(128)}, u32[]{:S(2)}) copy-start(s32[16]{0:T(128)} %param.16) | copy-start | bytes 196
  16.2 5.1 %copy-start.15 = (s32[16,1]{0,1:T(1,128)S(1)}, s32[16,1]{0,1:T(1,128)}, u32[]{:S(2)}) copy-start(s32[16,1]{0,1:T(1,128)} %param.15) | copy-start | bytes 196
  16.2 5.2 %copy-start.12 = (f32[1,2]{1,0:T(1,128)S(1)}, f32[1,2]{1,0:T(1,128)}, u32[]{:S(2)}) copy-start(f32[1,2]{1,0:T(1,128)} %param.19) | copy-start | bytes 28
  63.7 28.0 %all-to-all-start.1 = ((f32[16,16,384]{2,1,0:T(8,128)}), f32[16,16,384]{2,1,0:T(8,128)S(1)}, u32[]{:S(2)}, u32[]{:S(2)}) async-start(f32[16,16,384]{2,1,0:T(8,128)} %broadcast_in_dim.23), calls=%async_computation.1 | async-start | bytes 786432 | tf_op jit(solution)/shard_map/all_to_all | solution.py:396
  73.0 2.3 copy-start.6
  75.3 1.9 copy-start.2
  75.3 1.9 copy-start.3
  91.7 7.0 %copy-start.10 = (f32[128,256]{1,0:T(8,128)S(1)}, f32[128,256]{1,0:T(8,128)}, u32[]{:S(2)}) copy-start(f32[128,256]{1,0:T(8,128)} %constant.173) | copy-start | bytes 393220
  91.7 7.4 %copy-start.9 = (f32[128,256]{1,0:T(8,128)S(1)}, f32[128,256]{1,0:T(8,128)}, u32[]{:S(2)}) copy-start(f32[128,256]{1,0:T(8,128)} %constant.174) | copy-start | bytes 393220
  91.7 98.6 %all-to-all-start.3 = ((f32[16,2,128,256]{3,2,1,0:T(8,128)}), f32[16,2,128,256]{3,2,1,0:T(8,128)}, u32[]{:S(2)}, u32[]{:S(2)}) async-start(f32[16,2,128,256]{3,2,1,0:T(8,128)} %move_rows_source.1), calls=%async_computation.3 | async-start | bytes 8388608 | tf_op jit(solution)/shard_map/all_to_all | solution.py:432
  114.9 80.3 %copy-start.13 = (f32[1,2]{1,0:T(1,128)S(1)}, f32[1,2]{1,0:T(1,128)}, u32[]{:S(2)}) copy-start(f32[1,2]{1,0:T(1,128)} %param.19) | copy-start | bytes 28
  114.9 80.9 %copy-start = (s32[1,128,2048]{2,1,0:T(8,128)S(1)}, s32[1,128,2048]{2,1,0:T(8,128)}, u32[]{:S(2)}) copy-start(s32[1,128,2048]{2,1,0:T(8,128)} %param.18) | copy-start | bytes 3145732
  114.9 80.9 %copy-start.4 = (bf16[2,256,256]{2,1,0:T(8,128)(2,1)S(1)}, bf16[2,256,256]{2,1,0:T(8,128)(2,1)}, u32[]{:S(2)}) copy-start(bf16[2,256,256]{2,1,0:T(8,128)(2,1)} %constant.172.table) | copy-start | bytes 786436
  190.3 97.4 %all-to-all-start.2 = ((f32[16,2,128,256]{3,2,1,0:T(8,128)}), f32[16,2,128,256]{3,2,1,0:T(8,128)}, u32[]{:S(2)}, u32[]{:S(2)}) async-start(f32[16,2,128,256]{3,2,1,0:T(8,128)} %move_rows_received.1), calls=%async_computation.2 | async-start | bytes 8388608 | tf_op jit(solution)/shard_map/all_to_all | solution.py:432
  195.8 7.5 %copy-start.8 = (f32[1,128,2048]{2,1,0:T(8,128)S(1)}, f32[1,128,2048]{2,1,0:T(8,128)}, u32[]{:S(2)}) copy-start(f32[1,128,2048]{2,1,0:T(8,128)} %param.17) | copy-start | bytes 3145732

commit v3 on v2

--- a/solution.py
+++ b/solution.py
@@ -382,6 +382,9 @@
         ],
         axis=1,
     )
+    copies = jnp.broadcast_to(packed[None], (lanes,) + packed.shape)
+    packed = lax.all_to_all(copies, "lat", split_axis=0, concat_axis=0, tiled=True)
+
     spectrum = pl.pallas_call(
         forward_columns,
         out_shape=f32(INNER, rows, 2 * RADIX),
@@ -390,11 +393,9 @@
         cost_estimate=cost(2**23),
         name="forward_columns",
     )(source_field[:, 0], right_forward, twist)
+    packed, spectrum = lax.optimization_barrier((packed, spectrum))
+    packed = packed.reshape(lanes * count, 3 * width)
     source_part = lax.all_to_all(spectrum, "lat", split_axis=0, concat_axis=0, tiled=True)
-    packed, source_part = lax.optimization_barrier((packed, source_part))
-    copies = jnp.broadcast_to(packed[None], (lanes,) + packed.shape)
-    packed = lax.all_to_all(copies, "lat", split_axis=0, concat_axis=0, tiled=True)
-    packed = packed.reshape(lanes * count, 3 * width)
 
     step = 2.0 * math.pi / (LENGTH * SPACING) * DEPTH_STEP
     number = jnp.arange(LENGTH, dtype=jnp.int32)
@@ -431,8 +432,6 @@
     def send_back(moved):
         return lax.all_to_all(moved, "lat", split_axis=0, concat_axis=0, tiled=True)
 
-    packed, moved = lax.optimization_barrier((packed, propagate(source_part, -1.0, "source")))
-    source_back = send_back(moved)
 
     target = jnp.round(packed[:, 2 * width]).astype(jnp.int32)
     row, place = target // per_row, target % per_row
@@ -479,16 +478,21 @@
             name="backward_columns_" + label,
         )(back, chosen, right_backward, twist, *other)
 
-    received_back = send_back(propagate(received_part, 1.0, "received"))
-    source = restore(source_back, "source")
+    moved = propagate(received_part, 1.0, "received")
+    moved, source_part = lax.optimization_barrier((moved, source_part))
+    received_back = send_back(moved)
+    moved = propagate(source_part, -1.0, "source")
+    moved, received_back = lax.optimization_barrier((moved, received_back))
+    source_back = send_back(moved)
+    received = restore(received_back, "received")
     speed = jnp.where(chosen == 1, ref_slow[0, 1], ref_slow[0, 0])
     double = (2.0 * DEPTH_STEP) * omega[0] * (slowness[0] - speed)
     square = double * double
     cosine, sine = series(square, 0), double * series(square, 1)
-    turned_source = jnp.stack(
-        [source[0] * cosine + source[1] * sine, source[1] * cosine - source[0] * sine]
-    )
-    return restore(received_back, "image", turned_source)[None]
+    turned = jnp.stack(
+        [received[0] * cosine - received[1] * sine, received[1] * cosine + received[0] * sine]
+    )
+    return restore(source_back, "image", turned)[None]
 
 
 def solution(mesh):

time: 297 us -> 276 us (0.929)
  waiting for transfers between devices: 197 us -> 175 us
    all_to_all x1, waiting for transfers between devices: 40.1 us -> 13.9 us  [per_device(): lax.all_to_all(spectrum, 'lat', split_axis=0, concat_axis=0, tiled=True)]
    sub x0 -> x1, other arithmetic: none -> 3.05 us  [per_device(): received[0] * cosine - received[1] * sine]
    add x1 -> x0, other arithmetic: 3 us -> none  [per_device(): source[0] * cosine + source[1] * sine]
  transfers between devices with their start and end apart: 4 -> 4, of which waited for: 3 -> 4; matrix products, arithmetic and copies ran while one was open for 7% -> 8% of each run, Pallas kernels for 12% -> 15%
where the time goes in v3:
time: 276 us; the launch traced here: 275 us
  waiting for transfers between devices  175 us (63%)
  Pallas kernels  50.2 us (18%)
  starting transfers between devices  21.4 us (8%)
  other arithmetic  13.5 us (5%)
  local copies, waits for them, and re-layouts  12.2 us (4%)
    all_to_all x2, waiting for transfers between devices, send_back(): return lax.all_to_all(moved, 'lat', split_axis=0, concat_axis=0, tiled=True)  159 us
    pallas_call x2, Pallas kernels, propagate(): pl.pallas_call(partial(move_rows, sense), out_shape=f32(INNER, NREF, RADI...  28.7 us
    pallas_call x2, Pallas kernels, restore(): pl.pallas_call(backward_columns, grid=(rows // share,), in_specs=[pl.Bloc...  15.7 us
    all_to_all x1, waiting for transfers between devices, per_device(): lax.all_to_all(spectrum, 'lat', split_axis=0, concat_axis=0, tiled=True)  13.9 us
    all_to_all x2, starting transfers between devices, send_back(): return lax.all_to_all(moved, 'lat', split_axis=0, concat_axis=0, tiled=True)  9.79 us
    all_to_all x1, starting transfers between devices, per_device(): lax.all_to_all(copies, 'lat', split_axis=0, concat_axis=0, tiled=True)  6.55 us
    pallas_call x1, Pallas kernels, per_device(): pl.pallas_call(forward_columns, out_shape=f32(INNER, rows, 2 * RADIX), sc...  5.76 us
  transfers between devices with their start and end apart: 4, of which 4 were waited for; matrix products, arithmetic and copies ran while one was open for 8% of the time, Pallas kernels for 15%

profile of v3, /device:TPU:11, one launch (start us, length us, event | category | flops | bytes accessed | tf_op | source)
XLA Modules:
  0.0 275.0 jit_solution(13269449452305117815)
XLA Ops:
  2.3 6.6 %all-to-all-start = ((f32[16,16,384]{2,1,0:T(8,128)}), f32[16,16,384]{2,1,0:T(8,128)S(1)}, u32[]{:S(2)}, u32[]{:S(2)}) async-start(f32[16,16,384]{2,1,0:T(8,128)} %broadcast_in_dim.23), calls=%async_computation | async-start | bytes 786432 | tf_op jit(solution)/shard_map/all_to_all | solution.py:386
  9.5 0.9 copy-done.7
  10.5 5.8 %forward_columns.1 = f32[16,128,256]{2,1,0:T(8,128)S(1)} custom-call(f32[2,128,2048]{2,1,0:T(8,128)} %bitcast.43, bf16[2,256,256]{2,1,0:T(8,128)(2,1)S(1)} %copy-done.7, f32[2,16,128]{2,1,0:T(8,128)S(1)} %copy-done.5), custom_call_target="tpu_custom_call" | custom-call | flops 2000000000 | bytes 8388608 | tf_op jit(solution)/shard_map/forward_columns/pallas_call | solution.py:388
  16.3 1.3 copy-done.1
  17.6 2.0 all-to-all-done
  19.6 5.1 %all-to-all-start.1 = ((f32[16,128,256]{2,1,0:T(8,128)}), f32[16,128,256]{2,1,0:T(8,128)S(1)}, u32[]{:S(2)}, u32[]{:S(2)}) async-start(f32[16,128,256]{2,1,0:T(8,128)} %copy-done.1), calls=%async_computation.1 | async-start | bytes 4194304 | tf_op jit(solution)/shard_map/all_to_all | solution.py:398
  24.7 1.0 copy.15
  25.8 2.2 add.494
  28.0 1.8 add.495
  31.2 1.3 broadcast_add_fusion
  32.5 4.4 %fusion.31 = (f32[2,1,8,128,256]{4,3,2,1,0:T(8,128)S(1)}, f32[2,1,8,128,256]{4,3,2,1,0:T(8,128)S(1)}) fusion(f32[8,128,256]{2,1,0:T(8,128)S(1)} %broadcast_add_fusion, f32[2]{0:T(128)S(1)} %multiply_bitcast_fusion.1, f32[]{:T(128)S(6)} %sign.14), kind=kLoop, calls=%fused_computation.34 | loop fusion | flops 25690112 | bytes 5242892 | tf_op jit(solution)/shard_map/mul | solution.py:413
  36.9 2.3 pad_maximum_fusion.factor
  40.9 1.1 fusion.49
  42.0 1.9 broadcast_in_dim.51.twist
  43.9 14.3 %move_rows_received.1 = f32[16,2,128,256]{3,2,1,0:T(8,128)} custom-call(f32[16,128,256]{2,1,0:T(8,128)S(1)} %bitcast.36, f32[2,2,8,128,256]{4,3,2,1,0:T(8,128)} %pad_maximum_fusion.factor, bf16[2,256,256]{2,1,0:T(8,128)(2,1)S(1)} %copy-done.2, bf16[2,256,256]{2,1,0:T(8,128)(2,1)S(1)} %copy-done.3, f32[2,16,128,128]{3,2,1,0:T(8,128)} %broadcast_in_dim.51.twist), custom_call_target="tpu_custom_call" | custom-call | flops 2000000000 | bytes 33554432 | tf_op jit(solution)/shard_map/move_rows_received/pallas_call | solution.py:420
  58.2 13.9 %all-to-all-done.1.data = f32[16,128,256]{2,1,0:T(8,128)S(1)} async-done(((f32[16,128,256]{2,1,0:T(8,128)}), f32[16,128,256]{2,1,0:T(8,128)S(1)}, u32[]{:S(2)}, u32[]{:S(2)}) %all-to-all-start.1) | async-done | bytes 2097184 | tf_op jit(solution)/shard_map/all_to_all | solution.py:398
  72.1 4.9 %all-to-all-start.2 = ((f32[16,2,128,256]{3,2,1,0:T(8,128)}), f32[16,2,128,256]{3,2,1,0:T(8,128)}, u32[]{:S(2)}, u32[]{:S(2)}) async-start(f32[16,2,128,256]{3,2,1,0:T(8,128)} %move_rows_received.1), calls=%async_computation.2 | async-start | bytes 8388608 | tf_op jit(solution)/shard_map/all_to_all | solution.py:433
  77.0 14.4 %move_rows_source.1 = f32[16,2,128,256]{3,2,1,0:T(8,128)} custom-call(f32[16,128,256]{2,1,0:T(8,128)S(1)} %all-to-all-done.1.data, f32[2,2,8,128,256]{4,3,2,1,0:T(8,128)} %pad_maximum_fusion.factor, bf16[2,256,256]{2,1,0:T(8,128)(2,1)S(1)} %copy-done.2, bf16[2,256,256]{2,1,0:T(8,128)(2,1)S(1)} %copy-done.3, f32[2,16,128,128]{3,2,1,0:T(8,128)} %broadcast_in_dim.51.twist), custom_call_target="tpu_custom_call" | custom-call | flops 2000000000 | bytes 33554432 | tf_op jit(solution)/shard_map/move_rows_source/pallas_call | solution.py:420
  91.4 78.0 %all-to-all-done.2.data = f32[16,2,128,256]{3,2,1,0:T(8,128)} async-done(((f32[16,2,128,256]{3,2,1,0:T(8,128)}), f32[16,2,128,256]{3,2,1,0:T(8,128)}, u32[]{:S(2)}, u32[]{:S(2)}) %all-to-all-start.2) | async-done | bytes 4194336 | tf_op jit(solution)/shard_map/all_to_all | solution.py:433
  169.4 4.9 %all-to-all-start.3 = ((f32[16,2,128,256]{3,2,1,0:T(8,128)}), f32[16,2,128,256]{3,2,1,0:T(8,128)}, u32[]{:S(2)}, u32[]{:S(2)}) async-start(f32[16,2,128,256]{3,2,1,0:T(8,128)} %move_rows_source.1), calls=%async_computation.3 | async-start | bytes 8388608 | tf_op jit(solution)/shard_map/all_to_all | solution.py:433
  174.9 7.5 %backward_columns_received.1 = f32[2,128,2048]{2,1,0:T(8,128)S(1)} custom-call(f32[16,2,128,256]{3,2,1,0:T(8,128)} %all-to-all-done.2.data, s32[128,2048]{1,0:T(8,128)S(1)} %bitcast.34, bf16[2,256,256]{2,1,0:T(8,128)(2,1)S(1)} %copy-done.4, f32[2,16,128]{2,1,0:T(8,128)S(1)} %copy-done.6), custom_call_target="tpu_custom_call" | custom-call | flops 2000000000 | bytes 16777216 | tf_op jit(solution)/shard_map/backward_columns_received/pallas_call | solution.py:460
  182.5 3.1 %multiply_subtract_fusion = (f32[1,128,2048]{2,1,0:T(8,128)S(1)}, f32[1,128,2048]{2,1,0:T(8,128)S(1)}) fusion(f32[2,128,2048]{2,1,0:T(8,128)S(1)} %backward_columns_received.1, f32[1,128,2048]{2,1,0:T(8,128)S(1)} %copy-done.8, f32[]{:T(128)} %bitcast.12, f32[]{:T(128)} %bitcast.11, s32[1,128,2048]{2,1,0:T(8,128)S(1)} %copy-done, f32[]{:T(128)S(6)} %mul_shard_map.3), kind=kLoop, calls=%fused_computation.57 | loop fusion | flops 13631488 | bytes 6291468 | tf_op jit(solution)/shard_map/sub | solution.py:493
  185.7 81.1 %all-to-all-done.3.data = f32[16,2,128,256]{3,2,1,0:T(8,128)} async-done(((f32[16,2,128,256]{3,2,1,0:T(8,128)}), f32[16,2,128,256]{3,2,1,0:T(8,128)}, u32[]{:S(2)}, u32[]{:S(2)}) %all-to-all-start.3) | async-done | bytes 4194336 | tf_op jit(solution)/shard_map/all_to_all | solution.py:433
  266.8 8.2 %backward_columns_image.1 = f32[128,2048]{1,0:T(8,128)} custom-call(f32[16,2,128,256]{3,2,1,0:T(8,128)} %all-to-all-done.3.data, s32[128,2048]{1,0:T(8,128)S(1)} %bitcast.35, bf16[2,256,256]{2,1,0:T(8,128)(2,1)S(1)} %copy-done.4, f32[2,16,128]{2,1,0:T(8,128)S(1)} %copy-done.6, f32[2,128,2048]{2,1,0:T(8,128)S(1)} %pad_maximum_fusion.1.rest_0_), custom_call_target="tpu_custom_call" | custom-call | flops 2000000000 | bytes 16777216 | tf_op jit(solution)/shard_map/backward_columns_image/pallas_call | solution.py:460
  (41 shorter events, 6.1 us)
Async XLA Ops:
  2.3 17.3 %all-to-all-start = ((f32[16,16,384]{2,1,0:T(8,128)}), f32[16,16,384]{2,1,0:T(8,128)S(1)}, u32[]{:S(2)}, u32[]{:S(2)}) async-start(f32[16,16,384]{2,1,0:T(8,128)} %broadcast_in_dim.23), calls=%async_computation | async-start | bytes 786432 | tf_op jit(solution)/shard_map/all_to_all | solution.py:386
  8.8 0.7 copy-start.5
  9.5 0.9 copy-start.7
  16.2 1.3 copy-start.1
  19.6 52.5 %all-to-all-start.1 = ((f32[16,128,256]{2,1,0:T(8,128)}), f32[16,128,256]{2,1,0:T(8,128)S(1)}, u32[]{:S(2)}, u32[]{:S(2)}) async-start(f32[16,128,256]{2,1,0:T(8,128)} %copy-done.1), calls=%async_computation.1 | async-start | bytes 4194304 | tf_op jit(solution)/shard_map/all_to_all | solution.py:398
  24.7 5.7 %copy-start.6 = (f32[2,16,128]{2,1,0:T(8,128)S(1)}, f32[2,16,128]{2,1,0:T(8,128)}, u32[]{:S(2)}) copy-start(f32[2,16,128]{2,1,0:T(8,128)} %constant.138.clone.twist) | copy-start | bytes 49156
  36.9 3.1 %copy-start.10 = (f32[128,256]{1,0:T(8,128)S(1)}, f32[128,256]{1,0:T(8,128)}, u32[]{:S(2)}) copy-start(f32[128,256]{1,0:T(8,128)} %constant.173) | copy-start | bytes 393220
  36.9 3.6 %copy-start.9 = (f32[128,256]{1,0:T(8,128)S(1)}, f32[128,256]{1,0:T(8,128)}, u32[]{:S(2)}) copy-start(f32[128,256]{1,0:T(8,128)} %constant.174) | copy-start | bytes 393220
  40.9 3.0 %copy-start.2 = (bf16[2,256,256]{2,1,0:T(8,128)(2,1)S(1)}, bf16[2,256,256]{2,1,0:T(8,128)(2,1)}, u32[]{:S(2)}) copy-start(bf16[2,256,256]{2,1,0:T(8,128)(2,1)} %constant.158.forward) | copy-start | bytes 786436
  40.9 3.0 %copy-start.3 = (bf16[2,256,256]{2,1,0:T(8,128)(2,1)S(1)}, bf16[2,256,256]{2,1,0:T(8,128)(2,1)}, u32[]{:S(2)}) copy-start(bf16[2,256,256]{2,1,0:T(8,128)(2,1)} %constant.165.backward) | copy-start | bytes 786436
  72.1 97.4 %all-to-all-start.2 = ((f32[16,2,128,256]{3,2,1,0:T(8,128)}), f32[16,2,128,256]{3,2,1,0:T(8,128)}, u32[]{:S(2)}, u32[]{:S(2)}) async-start(f32[16,2,128,256]{3,2,1,0:T(8,128)} %move_rows_received.1), calls=%async_computation.2 | async-start | bytes 8388608 | tf_op jit(solution)/shard_map/all_to_all | solution.py:433
  91.4 82.9 %copy-start.11 = (f32[1,2]{1,0:T(1,128)S(1)}, f32[1,2]{1,0:T(1,128)}, u32[]{:S(2)}) copy-start(f32[1,2]{1,0:T(1,128)} %param.19) | copy-start | bytes 28
  91.4 83.5 %copy-start = (s32[1,128,2048]{2,1,0:T(8,128)S(1)}, s32[1,128,2048]{2,1,0:T(8,128)}, u32[]{:S(2)}) copy-start(s32[1,128,2048]{2,1,0:T(8,128)} %param.18) | copy-start | bytes 3145732
  91.4 83.5 %copy-start.4 = (bf16[2,256,256]{2,1,0:T(8,128)(2,1)S(1)}, bf16[2,256,256]{2,1,0:T(8,128)(2,1)}, u32[]{:S(2)}) copy-start(bf16[2,256,256]{2,1,0:T(8,128)(2,1)} %constant.172.table) | copy-start | bytes 786436
  169.4 97.4 %all-to-all-start.3 = ((f32[16,2,128,256]{3,2,1,0:T(8,128)}), f32[16,2,128,256]{3,2,1,0:T(8,128)}, u32[]{:S(2)}, u32[]{:S(2)}) async-start(f32[16,2,128,256]{3,2,1,0:T(8,128)} %move_rows_source.1), calls=%async_computation.3 | async-start | bytes 8388608 | tf_op jit(solution)/shard_map/all_to_all | solution.py:433
  174.9 7.5 %copy-start.8 = (f32[1,128,2048]{2,1,0:T(8,128)S(1)}, f32[1,128,2048]{2,1,0:T(8,128)}, u32[]{:S(2)}) copy-start(f32[1,128,2048]{2,1,0:T(8,128)} %param.17) | copy-start | bytes 3145732

commit v4 on v3

--- a/solution.py
+++ b/solution.py
@@ -314,14 +314,14 @@
     rows = data.shape[2]
     for which in range(NREF):
         flat = data[:, which].reshape(INNER * rows, 2 * RADIX)
-        work[...] = right_product(flat, table).reshape(INNER, rows, 2 * RADIX)
-
-        @pl.loop(0, rows // 8)
+        work[which] = right_product(flat, table).reshape(INNER, rows, 2 * RADIX)
+
+        @pl.loop(0, rows // 8, unroll=True)
         def _(i):
             here = row_chunk(i)
             values = []
             for c in range(INNER):
-                re, im = work[c, here, :RADIX], work[c, here, RADIX:]
+                re, im = work[which, c, here, :RADIX], work[which, c, here, RADIX:]
                 tr, ti = twist[0, c : c + 1, :], twist[1, c : c + 1, :]
                 values.append((re * tr + im * ti, im * tr - re * ti))
             for a, (re, im) in enumerate(butterflies(values, 1.0)):
@@ -363,6 +363,7 @@
     columns = source_field.shape[3]
     width = rec_blocks.shape[3]
     fits = lanes == INNER and rows == RADIX and columns == LENGTH and width == RADIX
+    fits = fits and rec_blocks.shape[0] <= RADIX
     if not fits or rec_blocks.shape[2] != 1 or source_field.shape[1] != 1:
         return general(
             source_field, rec_blocks, dest_device, dest_bin, slowness, ref_index, ref_slow, omega
@@ -377,10 +378,10 @@
     target = dest_device[:, 0] * (rows * per_row) + dest_bin
     packed = jnp.concatenate(
         [
-            rec_blocks.reshape(count, 2 * width),
-            jnp.broadcast_to(target.astype(jnp.float32)[:, None], (count, width)),
+            rec_blocks.reshape(2 * count, width),
+            jnp.pad(target.astype(jnp.float32), (0, width - count))[None],
         ],
-        axis=1,
+        axis=0,
     )
     copies = jnp.broadcast_to(packed[None], (lanes,) + packed.shape)
     packed = lax.all_to_all(copies, "lat", split_axis=0, concat_axis=0, tiled=True)
@@ -394,7 +395,7 @@
         name="forward_columns",
     )(source_field[:, 0], right_forward, twist)
     packed, spectrum = lax.optimization_barrier((packed, spectrum))
-    packed = packed.reshape(lanes * count, 3 * width)
+    blocks = packed[:, : 2 * count].reshape(lanes * count, 2 * width)
     source_part = lax.all_to_all(spectrum, "lat", split_axis=0, concat_axis=0, tiled=True)
 
     step = 2.0 * math.pi / (LENGTH * SPACING) * DEPTH_STEP
@@ -433,14 +434,14 @@
         return lax.all_to_all(moved, "lat", split_axis=0, concat_axis=0, tiled=True)
 
 
-    target = jnp.round(packed[:, 2 * width]).astype(jnp.int32)
+    target = jnp.round(packed[:, 2 * count, :count].reshape(-1)).astype(jnp.int32)
     row, place = target // per_row, target % per_row
     own = lax.dynamic_slice_in_dim(twist, me, 1, axis=1)[:, 0]
     turn = (place * me % INNER).astype(jnp.float32) * (-2.0 * math.pi / INNER)
     turn_real, turn_imag = jnp.cos(turn)[:, None], jnp.sin(turn)[:, None]
     weight_real = turn_real * own[0] - turn_imag * own[1]
     weight_imag = turn_real * own[1] + turn_imag * own[0]
-    real, imag = packed[:, :width], packed[:, width : 2 * width]
+    real, imag = blocks[:, :width], blocks[:, width:]
     turned = jnp.concatenate(
         [real * weight_real - imag * weight_imag, real * weight_imag + imag * weight_real], axis=1
     )
@@ -470,7 +471,7 @@
             out_specs=plane if other else fields,
             out_shape=f32(rows, columns) if other else f32(2, rows, columns),
             scratch_shapes=[
-                pltpu.VMEM((INNER, share, 2 * RADIX), jnp.float32),
+                pltpu.VMEM((NREF, INNER, share, 2 * RADIX), jnp.float32),
                 pltpu.VMEM((2, share, columns), jnp.float32),
             ],
             compiler_params=PARAMS,

time: 276 us -> 272 us (0.986)
  Pallas kernels: 50.2 us -> 45.6 us
    pallas_call x2, Pallas kernels: 15.7 us -> 11.1 us  [restore(): pl.pallas_call(backward_columns, grid=(rows // share,), in_specs=[pl.Bloc...]
where the time goes in v4:
time: 272 us
  waiting for transfers between devices  177 us (65%)
  Pallas kernels  45.6 us (17%)
  starting transfers between devices  21.8 us (8%)
  other arithmetic  12.8 us (5%)
  local copies, waits for them, and re-layouts  11.5 us (4%)
    all_to_all x2, waiting for transfers between devices, send_back(): return lax.all_to_all(moved, 'lat', split_axis=0, concat_axis=0, tiled=True)  161 us
    pallas_call x2, Pallas kernels, propagate(): pl.pallas_call(partial(move_rows, sense), out_shape=f32(INNER, NREF, RADI...  28.7 us
    all_to_all x1, waiting for transfers between devices, per_device(): lax.all_to_all(spectrum, 'lat', split_axis=0, concat_axis=0, tiled=True)  14.9 us
    pallas_call x2, Pallas kernels, restore(): pl.pallas_call(backward_columns, grid=(rows // share,), in_specs=[pl.Bloc...  11.1 us
    all_to_all x2, starting transfers between devices, send_back(): return lax.all_to_all(moved, 'lat', split_axis=0, concat_axis=0, tiled=True)  9.82 us
    all_to_all x1, starting transfers between devices, per_device(): lax.all_to_all(copies, 'lat', split_axis=0, concat_axis=0, tiled=True)  6.55 us
    pallas_call x1, Pallas kernels, per_device(): pl.pallas_call(forward_columns, out_shape=f32(INNER, rows, 2 * RADIX), sc...  5.76 us
  transfers between devices with their start and end apart: 4, of which 4 were waited for; matrix products, arithmetic and copies ran while one was open for 8% of the time, Pallas kernels for 15%

profile of v4, /device:TPU:11, one launch (start us, length us, event | category | flops | bytes accessed | tf_op | source)
XLA Modules:
  0.0 271.6 jit_solution(6825982421628283039)
XLA Ops:
  1.4 0.7 broadcast_in_dim.45
  2.2 6.6 %all-to-all-start = ((f32[16,33,128]{2,1,0:T(8,128)}), f32[16,33,128]{2,1,0:T(8,128)S(1)}, u32[]{:S(2)}, u32[]{:S(2)}) async-start(f32[16,33,128]{2,1,0:T(8,128)} %broadcast_in_dim.45), calls=%async_computation | async-start | bytes 655360 | tf_op jit(solution)/shard_map/all_to_all | solution.py:387
  9.4 0.9 copy-done.7
  10.4 5.8 %forward_columns.1 = f32[16,128,256]{2,1,0:T(8,128)S(1)} custom-call(f32[2,128,2048]{2,1,0:T(8,128)} %bitcast.34, bf16[2,256,256]{2,1,0:T(8,128)(2,1)S(1)} %copy-done.7, f32[2,16,128]{2,1,0:T(8,128)S(1)} %copy-done.5), custom_call_target="tpu_custom_call" | custom-call | flops 2000000000 | bytes 8388608 | tf_op jit(solution)/shard_map/forward_columns/pallas_call | solution.py:389
  16.2 1.3 copy-done.1
  18.1 5.4 %all-to-all-start.1 = ((f32[16,128,256]{2,1,0:T(8,128)}), f32[16,128,256]{2,1,0:T(8,128)S(1)}, u32[]{:S(2)}, u32[]{:S(2)}) async-start(f32[16,128,256]{2,1,0:T(8,128)} %copy-done.1), calls=%async_computation.1 | async-start | bytes 4194304 | tf_op jit(solution)/shard_map/all_to_all | solution.py:399
  23.6 1.0 copy.14
  24.6 2.2 add.506
  26.8 1.8 add.507
  29.4 1.3 broadcast_add_fusion
  30.7 4.4 %fusion.31 = (f32[2,1,8,128,256]{4,3,2,1,0:T(8,128)S(1)}, f32[2,1,8,128,256]{4,3,2,1,0:T(8,128)S(1)}) fusion(f32[8,128,256]{2,1,0:T(8,128)S(1)} %broadcast_add_fusion, f32[2]{0:T(128)S(1)} %multiply_bitcast_fusion.1, f32[]{:T(128)S(6)} %sign.14), kind=kLoop, calls=%fused_computation.34 | loop fusion | flops 25690112 | bytes 5242892 | tf_op jit(solution)/shard_map/mul | solution.py:414
  35.1 2.3 pad_maximum_fusion.factor
  38.7 1.1 fusion.49
  39.8 1.9 broadcast_in_dim.48.twist
  41.7 14.3 %move_rows_received.1 = f32[16,2,128,256]{3,2,1,0:T(8,128)} custom-call(f32[16,128,256]{2,1,0:T(8,128)S(1)} %bitcast.32, f32[2,2,8,128,256]{4,3,2,1,0:T(8,128)} %pad_maximum_fusion.factor, bf16[2,256,256]{2,1,0:T(8,128)(2,1)S(1)} %copy-done.2, bf16[2,256,256]{2,1,0:T(8,128)(2,1)S(1)} %copy-done.3, f32[2,16,128,128]{3,2,1,0:T(8,128)} %broadcast_in_dim.48.twist), custom_call_target="tpu_custom_call" | custom-call | flops 2000000000 | bytes 33554432 | tf_op jit(solution)/shard_map/move_rows_received/pallas_call | solution.py:421
  56.0 14.9 %all-to-all-done.1.data = f32[16,128,256]{2,1,0:T(8,128)S(1)} async-done(((f32[16,128,256]{2,1,0:T(8,128)}), f32[16,128,256]{2,1,0:T(8,128)S(1)}, u32[]{:S(2)}, u32[]{:S(2)}) %all-to-all-start.1) | async-done | bytes 2097184 | tf_op jit(solution)/shard_map/all_to_all | solution.py:399
  70.9 4.9 %all-to-all-start.2 = ((f32[16,2,128,256]{3,2,1,0:T(8,128)}), f32[16,2,128,256]{3,2,1,0:T(8,128)}, u32[]{:S(2)}, u32[]{:S(2)}) async-start(f32[16,2,128,256]{3,2,1,0:T(8,128)} %move_rows_received.1), calls=%async_computation.2 | async-start | bytes 8388608 | tf_op jit(solution)/shard_map/all_to_all | solution.py:434
  75.8 14.4 %move_rows_source.1 = f32[16,2,128,256]{3,2,1,0:T(8,128)} custom-call(f32[16,128,256]{2,1,0:T(8,128)S(1)} %all-to-all-done.1.data, f32[2,2,8,128,256]{4,3,2,1,0:T(8,128)} %pad_maximum_fusion.factor, bf16[2,256,256]{2,1,0:T(8,128)(2,1)S(1)} %copy-done.2, bf16[2,256,256]{2,1,0:T(8,128)(2,1)S(1)} %copy-done.3, f32[2,16,128,128]{3,2,1,0:T(8,128)} %broadcast_in_dim.48.twist), custom_call_target="tpu_custom_call" | custom-call | flops 2000000000 | bytes 33554432 | tf_op jit(solution)/shard_map/move_rows_source/pallas_call | solution.py:421
  90.3 78.0 %all-to-all-done.2.data = f32[16,2,128,256]{3,2,1,0:T(8,128)} async-done(((f32[16,2,128,256]{3,2,1,0:T(8,128)}), f32[16,2,128,256]{3,2,1,0:T(8,128)}, u32[]{:S(2)}, u32[]{:S(2)}) %all-to-all-start.2) | async-done | bytes 4194336 | tf_op jit(solution)/shard_map/all_to_all | solution.py:434
  168.3 4.9 %all-to-all-start.3 = ((f32[16,2,128,256]{3,2,1,0:T(8,128)}), f32[16,2,128,256]{3,2,1,0:T(8,128)}, u32[]{:S(2)}, u32[]{:S(2)}) async-start(f32[16,2,128,256]{3,2,1,0:T(8,128)} %move_rows_source.1), calls=%async_computation.3 | async-start | bytes 8388608 | tf_op jit(solution)/shard_map/all_to_all | solution.py:434
  173.8 5.2 %backward_columns_received.1 = f32[2,128,2048]{2,1,0:T(8,128)S(1)} custom-call(f32[16,2,128,256]{3,2,1,0:T(8,128)} %all-to-all-done.2.data, s32[128,2048]{1,0:T(8,128)S(1)} %bitcast.30, bf16[2,256,256]{2,1,0:T(8,128)(2,1)S(1)} %copy-done.4, f32[2,16,128]{2,1,0:T(8,128)S(1)} %copy-done.6), custom_call_target="tpu_custom_call" | custom-call | flops 2000000000 | bytes 16777216 | tf_op jit(solution)/shard_map/backward_columns_received/pallas_call | solution.py:461
  179.0 3.0 %multiply_subtract_fusion = (f32[1,128,2048]{2,1,0:T(8,128)S(1)}, f32[1,128,2048]{2,1,0:T(8,128)S(1)}) fusion(f32[2,128,2048]{2,1,0:T(8,128)S(1)} %backward_columns_received.1, f32[1,128,2048]{2,1,0:T(8,128)S(1)} %copy-done.8, f32[]{:T(128)} %bitcast.13, f32[]{:T(128)} %bitcast.12, s32[1,128,2048]{2,1,0:T(8,128)S(1)} %copy-done, f32[]{:T(128)S(6)} %mul_shard_map.3), kind=kLoop, calls=%fused_computation.57 | loop fusion | flops 13631488 | bytes 6291468 | tf_op jit(solution)/shard_map/sub | solution.py:494
  182.2 83.5 %all-to-all-done.3.data = f32[16,2,128,256]{3,2,1,0:T(8,128)} async-done(((f32[16,2,128,256]{3,2,1,0:T(8,128)}), f32[16,2,128,256]{3,2,1,0:T(8,128)}, u32[]{:S(2)}, u32[]{:S(2)}) %all-to-all-start.3) | async-done | bytes 4194336 | tf_op jit(solution)/shard_map/all_to_all | solution.py:434
  265.7 5.9 %backward_columns_image.1 = f32[128,2048]{1,0:T(8,128)} custom-call(f32[16,2,128,256]{3,2,1,0:T(8,128)} %all-to-all-done.3.data, s32[128,2048]{1,0:T(8,128)S(1)} %bitcast.31, bf16[2,256,256]{2,1,0:T(8,128)(2,1)S(1)} %copy-done.4, f32[2,16,128]{2,1,0:T(8,128)S(1)} %copy-done.6, f32[2,128,2048]{2,1,0:T(8,128)S(1)} %pad_maximum_fusion.1.rest_0_), custom_call_target="tpu_custom_call" | custom-call | flops 2000000000 | bytes 16777216 | tf_op jit(solution)/shard_map/backward_columns_image/pallas_call | solution.py:461
  (44 shorter events, 4.8 us)
Async XLA Ops:
  2.2 15.9 %all-to-all-start = ((f32[16,33,128]{2,1,0:T(8,128)}), f32[16,33,128]{2,1,0:T(8,128)S(1)}, u32[]{:S(2)}, u32[]{:S(2)}) async-start(f32[16,33,128]{2,1,0:T(8,128)} %broadcast_in_dim.45), calls=%async_computation | async-start | bytes 655360 | tf_op jit(solution)/shard_map/all_to_all | solution.py:387
  8.7 0.7 copy-start.5
  9.4 0.9 copy-start.7
  16.1 1.3 copy-start.1
  18.1 52.8 %all-to-all-start.1 = ((f32[16,128,256]{2,1,0:T(8,128)}), f32[16,128,256]{2,1,0:T(8,128)S(1)}, u32[]{:S(2)}, u32[]{:S(2)}) async-start(f32[16,128,256]{2,1,0:T(8,128)} %copy-done.1), calls=%async_computation.1 | async-start | bytes 4194304 | tf_op jit(solution)/shard_map/all_to_all | solution.py:399
  23.6 5.7 %copy-start.6 = (f32[2,16,128]{2,1,0:T(8,128)S(1)}, f32[2,16,128]{2,1,0:T(8,128)}, u32[]{:S(2)}) copy-start(f32[2,16,128]{2,1,0:T(8,128)} %constant.139.clone.twist) | copy-start | bytes 49156
  23.6 5.8 %copy-start.11 = (f32[1,2]{1,0:T(1,128)S(1)}, f32[1,2]{1,0:T(1,128)}, u32[]{:S(2)}) copy-start(f32[1,2]{1,0:T(1,128)} %param.19) | copy-start | bytes 28
  35.1 2.7 copy-start.10
  35.1 3.1 %copy-start.9 = (f32[128,256]{1,0:T(8,128)S(1)}, f32[128,256]{1,0:T(8,128)}, u32[]{:S(2)}) copy-start(f32[128,256]{1,0:T(8,128)} %constant.177) | copy-start | bytes 393220
  38.7 3.0 %copy-start.2 = (bf16[2,256,256]{2,1,0:T(8,128)(2,1)S(1)}, bf16[2,256,256]{2,1,0:T(8,128)(2,1)}, u32[]{:S(2)}) copy-start(bf16[2,256,256]{2,1,0:T(8,128)(2,1)} %constant.161.forward) | copy-start | bytes 786436
  38.7 3.0 %copy-start.3 = (bf16[2,256,256]{2,1,0:T(8,128)(2,1)S(1)}, bf16[2,256,256]{2,1,0:T(8,128)(2,1)}, u32[]{:S(2)}) copy-start(bf16[2,256,256]{2,1,0:T(8,128)(2,1)} %constant.168.backward) | copy-start | bytes 786436
  70.9 97.4 %all-to-all-start.2 = ((f32[16,2,128,256]{3,2,1,0:T(8,128)}), f32[16,2,128,256]{3,2,1,0:T(8,128)}, u32[]{:S(2)}, u32[]{:S(2)}) async-start(f32[16,2,128,256]{3,2,1,0:T(8,128)} %move_rows_received.1), calls=%async_computation.2 | async-start | bytes 8388608 | tf_op jit(solution)/shard_map/all_to_all | solution.py:434
  90.2 83.5 %copy-start = (s32[1,128,2048]{2,1,0:T(8,128)S(1)}, s32[1,128,2048]{2,1,0:T(8,128)}, u32[]{:S(2)}) copy-start(s32[1,128,2048]{2,1,0:T(8,128)} %param.18) | copy-start | bytes 3145732
  90.3 83.5 %copy-start.4 = (bf16[2,256,256]{2,1,0:T(8,128)(2,1)S(1)}, bf16[2,256,256]{2,1,0:T(8,128)(2,1)}, u32[]{:S(2)}) copy-start(bf16[2,256,256]{2,1,0:T(8,128)(2,1)} %constant.175.table) | copy-start | bytes 786436
  168.3 97.4 %all-to-all-start.3 = ((f32[16,2,128,256]{3,2,1,0:T(8,128)}), f32[16,2,128,256]{3,2,1,0:T(8,128)}, u32[]{:S(2)}, u32[]{:S(2)}) async-start(f32[16,2,128,256]{3,2,1,0:T(8,128)} %move_rows_source.1), calls=%async_computation.3 | async-start | bytes 8388608 | tf_op jit(solution)/shard_map/all_to_all | solution.py:434
  173.8 5.2 %copy-start.8 = (f32[1,128,2048]{2,1,0:T(8,128)S(1)}, f32[1,128,2048]{2,1,0:T(8,128)}, u32[]{:S(2)}) copy-start(f32[1,128,2048]{2,1,0:T(8,128)} %param.17) | copy-start | bytes 3145732
